TPU v7x, 512 devices: a whole 4x8x8 slice. The times are simulated.
512 devices in a mesh: seq: 32 (over y_hi, z, core), tensor: 16 (over y_lo, x).
Axes of the slice: x: 4, y: 8 (y_hi: 2, y_lo: 4; y = y_hi * 4 + y_lo), z: 8, core: 2. Of those that a mesh axis runs over, the one named last changes fastest.
Arguments:
- tokens: bfloat16 [8192, 2304], P('seq'), may hold values from -6 to 6
- target: bfloat16 [8192, 2304], P('seq'), may hold values from -6 to 6
- segment_ids: int32 [8192], P('seq'), may hold values from 0 to 31, never falling along the last dimension, each value on 1 to 1024 neighbouring positions
- norm_gain: float32 [2304], replicated, may hold values from 0.1 to 1.9
- w_gate: bfloat16 [2304, 4608], P('seq', 'tensor'), may hold values from -0.125 to 0.125
- w_up: bfloat16 [2304, 4608], P('seq', 'tensor'), may hold values from -0.125 to 0.125
- w_down: bfloat16 [4608, 2304], P('tensor', 'seq'), may hold values from -0.09375 to 0.09375
- dir_gate: bfloat16 [2304, 4608], P('seq', 'tensor'), may hold values from -4 to 4
- dir_up: bfloat16 [2304, 4608], P('seq', 'tensor'), may hold values from -4 to 4
- dir_down: bfloat16 [4608, 2304], P('tensor', 'seq'), may hold values from -4 to 4
- ema_gate: float32 [2304, 4608], P('seq', 'tensor'), may hold values from 0.05 to 2
- ema_up: float32 [2304, 4608], P('seq', 'tensor'), may hold values from 0.05 to 2
- ema_down: float32 [4608, 2304], P('tensor', 'seq'), may hold values from 0.05 to 2
Outputs:
- new_gate: float32 [2304, 4608], P('seq', 'tensor')
- new_up: float32 [2304, 4608], P('seq', 'tensor')
- new_down: float32 [4608, 2304], P('tensor', 'seq')
Inputs may be any that keep to these rules, and one draw needn't show every extreme that they name: `segment_ids`: ids never fall along the pack; each of the 32 documents has 1 to 1024 tokens, and one has exactly 1024.
All inputs are finite; a program needn't handle non-finite values.
Results may differ from a plain program's by a relative error of at most 0.025.
Values may be sent and summed in bfloat16 or wider, within the bound.
No kernel may reach another device: no remote copies, remote signals or barrier semaphores. Data moves between devices by JAX's collectives and lax.ppermute only.
A program may use at most 64 MiB of HBM per device.

v0:
```python
import jax
import jax.numpy as jnp
from jax import lax
from jax.sharding import PartitionSpec as P

gelu_rate = 0.7978845608028654
gelu_cubic = 0.044715
beta_decay = 0.9
norm_eps = 1e-06


def gelu_parts(pre):
    inner = gelu_rate * (pre + gelu_cubic * pre * pre * pre)
    slope = gelu_rate * (1.0 + 3.0 * gelu_cubic * pre * pre)
    bend = 6.0 * gelu_rate * gelu_cubic * pre
    tanh_val = jnp.tanh(inner)
    sech_sq = 1.0 - tanh_val * tanh_val
    value = 0.5 * pre * (1.0 + tanh_val)
    first = 0.5 * (1.0 + tanh_val) + 0.5 * pre * sech_sq * slope
    second = sech_sq * (slope + 0.5 * pre * (bend - 2.0 * tanh_val * slope * slope))
    return (value, first, second)


def normalize(tokens, norm_gain):
    wide = tokens.astype(jnp.float32)
    scale = lax.rsqrt(jnp.mean(wide * wide, axis=1, keepdims=True) + norm_eps)
    return (wide * scale * norm_gain).astype(jnp.bfloat16)


def product(left, right):
    return jnp.dot(left, right, preferred_element_type=jnp.float32)


def against(left, right):
    return lax.dot_general(
        left, right, (((1,), (1,)), ((), ())), preferred_element_type=jnp.float32
    )


def over_tokens(left, right):
    return lax.dot_general(
        left, right, (((0,), (0,)), ((), ())), preferred_element_type=jnp.float32
    )


def out_grads(tokens, target, mixed, mixed_dot, lengths):
    residual = tokens.astype(jnp.float32) + mixed - target.astype(jnp.float32)
    grad_out = (residual / lengths[:, None]).astype(jnp.bfloat16)
    grad_out_dot = (mixed_dot / lengths[:, None]).astype(jnp.bfloat16)
    return (grad_out, grad_out_dot)


def second_order(grad_hidden, grad_hidden_dot, upper, upper_dot, value, first, second, gate_dot):
    grad_gate_dot = (
        (grad_hidden_dot * upper + grad_hidden * upper_dot) * first
        + grad_hidden * upper * second * gate_dot
    ).astype(jnp.bfloat16)
    grad_upper_dot = (grad_hidden_dot * value + grad_hidden * first * gate_dot).astype(jnp.bfloat16)
    return (grad_gate_dot, grad_upper_dot)


def blend(ema, probe, hvp):
    return beta_decay * ema + (1.0 - beta_decay) * (probe.astype(jnp.float32) * hvp)


def per_device(
    tokens,
    target,
    segment_ids,
    norm_gain,
    w_gate,
    w_up,
    w_down,
    dir_gate,
    dir_up,
    dir_down,
    ema_gate,
    ema_up,
    ema_down,
):
    normed = normalize(tokens, norm_gain)
    pieces = (
        lax.all_gather(w_gate, "seq", axis=0, tiled=True),
        lax.all_gather(w_up, "seq", axis=0, tiled=True),
        lax.all_gather(dir_gate, "seq", axis=0, tiled=True),
        lax.all_gather(dir_up, "seq", axis=0, tiled=True),
    )
    gate, upper, gate_dot, upper_dot = tuple((product(normed, piece) for piece in pieces))
    value, first, second = gelu_parts(gate)
    hidden = (value * upper).astype(jnp.bfloat16)
    hidden_dot = (first * gate_dot * upper + value * upper_dot).astype(jnp.bfloat16)
    labels = jnp.arange(lax.axis_size("seq"), dtype=jnp.int32)
    onehot = (segment_ids[:, None] == labels[None, :]).astype(jnp.float32)
    counts = lax.psum(jnp.sum(onehot, axis=0), "seq")
    lengths = jnp.dot(onehot, counts, precision=lax.Precision.HIGHEST)
    down_full, probe_full = (
        lax.all_gather(w_down, "seq", axis=1, tiled=True),
        lax.all_gather(dir_down, "seq", axis=1, tiled=True),
    )
    mixed_part = product(hidden, down_full)
    mixed_dot_part = product(hidden_dot, down_full) + product(hidden, probe_full)
    mixed, mixed_dot = (
        lax.psum(mixed_part.astype(jnp.bfloat16), "tensor").astype(jnp.float32),
        lax.psum(mixed_dot_part.astype(jnp.bfloat16), "tensor").astype(jnp.float32),
    )
    grad_out, grad_out_dot = out_grads(tokens, target, mixed, mixed_dot, lengths)
    grad_hidden = against(grad_out, down_full)
    grad_hidden_dot = against(grad_out_dot, down_full) + against(grad_out, probe_full)
    grad_gate_dot, grad_upper_dot = second_order(
        grad_hidden, grad_hidden_dot, upper, upper_dot, value, first, second, gate_dot
    )
    term_gate = over_tokens(normed, grad_gate_dot)
    term_up = over_tokens(normed, grad_upper_dot)
    term_down = over_tokens(hidden_dot, grad_out) + over_tokens(hidden, grad_out_dot)
    hvp_gate, hvp_up = (
        lax.psum_scatter(
            term_gate.astype(jnp.bfloat16), "seq", scatter_dimension=0, tiled=True
        ).astype(jnp.float32),
        lax.psum_scatter(
            term_up.astype(jnp.bfloat16), "seq", scatter_dimension=0, tiled=True
        ).astype(jnp.float32),
    )
    hvp_down = lax.psum_scatter(
        term_down.astype(jnp.bfloat16), "seq", scatter_dimension=1, tiled=True
    ).astype(jnp.float32)
    return (
        blend(ema_gate, dir_gate, hvp_gate),
        blend(ema_up, dir_up, hvp_up),
        blend(ema_down, dir_down, hvp_down),
    )


def solution(mesh):
    in_specs = (
        P("seq", None),
        P("seq", None),
        P("seq"),
        P(),
        P("seq", "tensor"),
        P("seq", "tensor"),
        P("tensor", "seq"),
        P("seq", "tensor"),
        P("seq", "tensor"),
        P("tensor", "seq"),
        P("seq", "tensor"),
        P("seq", "tensor"),
        P("tensor", "seq"),
    )
    out_specs = (P("seq", "tensor"), P("seq", "tensor"), P("tensor", "seq"))
    return jax.shard_map(
        per_device, mesh=mesh, in_specs=in_specs, out_specs=out_specs, check_vma=False
    )
```

profile of v0, /device:TPU:56, one launch (start us, length us, event | category | flops | bytes accessed | tf_op | source)
XLA Modules:
  0.0 1132.4 jit_solution(12601047903070680381)
XLA Ops:
  7.2 0.0 all-gather.9.cloned.1.call-start
  7.2 0.7 all-gather.9.cloned.1.call-update
  7.9 0.0 all-gather.7.cloned.1.call-start
  7.9 0.7 all-gather.7.cloned.1.call-update
  8.6 0.0 all-gather.11.cloned.1.call-start
  8.7 0.7 all-gather.11.cloned.1.call-update
  9.4 0.0 all-gather.13.cloned.1.call-start
  9.4 0.5 all-gather.13.cloned.1.call-update
  10.0 0.0 all-gather.15.cloned.1.call-start
  10.0 0.5 all-gather.15.cloned.1.call-update
  10.5 0.0 all-gather.17.cloned.1.call-start
  10.6 0.5 all-gather.17.cloned.1.call-update
  11.1 0.0 all-reduce.6.cloned.1.call-start
  11.2 1.6 fusion.2
  12.8 0.0 copy-start.2
  12.8 0.0 copy-start.12
  12.8 89.7 %all-gather.9.cloned.1.call-done = bf16[2304,288]{1,0:T(8,128)(2,1)} async-done(((bf16[72,288]{1,0:T(8,128)(2,1)}), bf16[2304,288]{1,0:T(8,128)(2,1)}) %all-gather.9.cloned.1.call-update) | async-done | bytes 1327120 | tf_op jit(solution)/shard_map/all_gather | solution.py:85
  102.5 2.7 fusion.45
  105.2 85.9 %all-gather.7.cloned.1.call-done = bf16[2304,288]{1,0:T(8,128)(2,1)} async-done(((bf16[72,288]{1,0:T(8,128)(2,1)}), bf16[2304,288]{1,0:T(8,128)(2,1)}) %all-gather.7.cloned.1.call-update) | async-done | bytes 1327120 | tf_op jit(solution)/shard_map/all_gather | solution.py:83
  191.1 2.3 fusion.47
  193.4 86.3 %all-gather.11.cloned.1.call-done = bf16[2304,288]{1,0:T(8,128)(2,1)} async-done(((bf16[72,288]{1,0:T(8,128)(2,1)}), bf16[2304,288]{1,0:T(8,128)(2,1)}) %all-gather.11.cloned.1.call-update) | async-done | bytes 1327120 | tf_op jit(solution)/shard_map/all_gather | solution.py:84
  279.7 2.3 fusion.43
  282.0 86.1 %all-gather.13.cloned.1.call-done = bf16[2304,288]{1,0:T(8,128)(2,1)} async-done(((bf16[72,288]{1,0:T(8,128)(2,1)}), bf16[2304,288]{1,0:T(8,128)(2,1)}) %all-gather.13.cloned.1.call-update) | async-done | bytes 1327120 | tf_op jit(solution)/shard_map/all_gather | solution.py:86
  368.1 3.2 add_convert_fusion.1
  371.3 85.2 %all-gather.15.cloned.1.call-done = bf16[288,2304]{0,1:T(8,128)(2,1)} async-done(((bf16[288,72]{0,1:T(8,128)(2,1)}), bf16[288,2304]{0,1:T(8,128)(2,1)}) %all-gather.15.cloned.1.call-update) | async-done | bytes 1327120 | tf_op jit(solution)/shard_map/all_gather | solution.py:97
  456.6 3.5 convolution_convert_fusion.2
  460.0 2.2 fusion.49
  462.3 82.7 %all-gather.17.cloned.1.call-done = bf16[288,2304]{0,1:T(8,128)(2,1)} async-done(((bf16[288,72]{0,1:T(8,128)(2,1)}), bf16[288,2304]{0,1:T(8,128)(2,1)}) %all-gather.17.cloned.1.call-update) | async-done | bytes 1327120 | tf_op jit(solution)/shard_map/all_gather | solution.py:98
  545.0 4.0 fusion.1
  549.0 0.0 all-reduce.6.cloned.1.call-update
  549.1 0.0 reduce-scatter.10.cloned.1.call-start
  549.1 0.6 copy-done.14
  549.7 0.1 convert_reduce_fusion
  549.8 91.0 %psum.22 = f32[32]{0:T(128)S(1)} all-reduce(f32[32]{0:T(128)S(1)} %convert_reduce_fusion), channel_id=1, replica_groups=mesh['seq'=32,'tensor'=16] {'seq'}, use_global_device_ids=true, to_apply=%region_3.0 | all-reduce | flops 32 | bytes 256 | tf_op jit(solution)/shard_map/psum | solution.py:94
  640.8 0.1 fusion.28
  640.9 76.2 %all-reduce.6.cloned.1.call-done = (bf16[256,2304]{1,0:T(8,128)(2,1)}, bf16[256,2304]{1,0:T(8,128)(2,1)}) async-done(((bf16[256,2304]{1,0:T(8,128)(2,1)}, bf16[256,2304]{1,0:T(8,128)(2,1)}), (bf16[256,2304]{1,0:T(8,128)(2,1)}, bf16[256,2304]{1,0:T(8,128)(2,1)})) %all-reduce.6.cloned.1.call-update) | async-done | bytes 2359312 | tf_op jit(solution)/shard_map/psum | solution.py:103
  717.2 2.5 fusion.7
  719.7 0.8 fusion.50
  720.4 0.5 copy-done.10
  720.9 0.8 fusion.38
  721.8 0.6 copy-done.1
  722.4 0.8 convolution_add_fusion.2
  723.2 0.5 copy-done.3
  723.7 0.1 copy-done.16
  723.7 0.1 copy-done.18
  723.8 0.1 copy-done.20
  723.9 0.1 copy-done.21
  724.0 2.4 convolution_convert_fusion.1
  726.4 0.0 reduce-scatter.10.cloned.1.call-update
  726.4 0.0 reduce-scatter.12.cloned.1.call-start
  726.4 3.3 convolution_convert_fusion
  729.7 0.0 reduce-scatter.12.cloned.1.call-update
  729.8 0.0 reduce-scatter.14.cloned.1.call-start
  729.8 0.8 fusion.51
  730.6 0.4 copy-done.11
  731.0 2.2 fusion
  733.2 0.0 copy-start.9
  733.2 0.0 reduce-scatter.14.cloned.1.call-update
  733.3 126.4 %reduce-scatter.10.cloned.1.call-done = bf16[72,288]{1,0:T(8,128)(2,1)} async-done(((bf16[2304,288]{1,0:T(8,128)(2,1)}), bf16[72,288]{1,0:T(8,128)(2,1)}) %reduce-scatter.10.cloned.1.call-update) | async-done | bytes 41488
  859.7 1.5 multiply_add_fusion.4
  861.2 130.8 %reduce-scatter.12.cloned.1.call-done = bf16[72,288]{1,0:T(8,128)(2,1)} async-done(((bf16[2304,288]{1,0:T(8,128)(2,1)}), bf16[72,288]{1,0:T(8,128)(2,1)}) %reduce-scatter.12.cloned.1.call-update) | async-done | bytes 41488
  992.0 1.5 multiply_add_fusion.3
  993.5 130.6 %reduce-scatter.14.cloned.1.call-done = bf16[288,72]{0,1:T(8,128)(2,1)} async-done(((bf16[288,2304]{0,1:T(8,128)(2,1)}), bf16[288,72]{0,1:T(8,128)(2,1)}) %reduce-scatter.14.cloned.1.call-update) | async-done | bytes 41488
  1124.1 1.5 multiply_add_fusion.2
  (33 shorter events, 0.1 us)
Async XLA Ops:
  7.2 95.4 %all-gather.9.cloned.1.call-start = ((), (), s32[]{:S(2)}) async-start(), calls=%async_computation.4 | async-start | bytes 1824768 | tf_op jit(solution)/shard_map/all_gather | solution.py:85
  7.9 183.2 %all-gather.7.cloned.1.call-start = ((), (), s32[]{:S(2)}) async-start(), calls=%async_computation.3 | async-start | bytes 1824768 | tf_op jit(solution)/shard_map/all_gather | solution.py:83
  8.6 271.1 %all-gather.11.cloned.1.call-start = ((), (), s32[]{:S(2)}) async-start(), calls=%async_computation.5 | async-start | bytes 1824768 | tf_op jit(solution)/shard_map/all_gather | solution.py:84
  9.4 358.8 %all-gather.13.cloned.1.call-start = ((), (), s32[]{:S(2)}) async-start(), calls=%async_computation.6 | async-start | bytes 1824768 | tf_op jit(solution)/shard_map/all_gather | solution.py:86
  10.0 446.6 %all-gather.15.cloned.1.call-start = ((), (), s32[]{:S(2)}) async-start(), calls=%async_computation.7 | async-start | bytes 1824768 | tf_op jit(solution)/shard_map/all_gather | solution.py:97
  10.5 534.5 %all-gather.17.cloned.1.call-start = ((), (), s32[]{:S(2)}) async-start(), calls=%async_computation.8 | async-start | bytes 1824768 | tf_op jit(solution)/shard_map/all_gather | solution.py:98
  11.1 706.1 %all-reduce.6.cloned.1.call-start = ((), (), s32[]{:S(2)}) async-start(), calls=%async_computation.12 | async-start | bytes 4718592 | tf_op jit(solution)/shard_map/psum | solution.py:103
  12.8 178.3 %copy-start.2 = (bf16[256,2304]{1,0:T(8,128)(2,1)S(1)}, bf16[256,2304]{1,0:T(8,128)(2,1)}, u32[]{:S(2)}) copy-start(bf16[256,2304]{1,0:T(8,128)(2,1)} %param.13) | copy-start | bytes 3538948
  12.8 178.3 %copy-start.12 = (f32[2304]{0:T(1024)S(1)}, f32[2304]{0:T(1024)}, u32[]{:S(2)}) copy-start(f32[2304]{0:T(1024)} %param.16) | copy-start | bytes 27652
  105.2 262.9 %copy-start.15 = (f32[256,288]{0,1:T(8,128)}, f32[256,288]{0,1:T(8,128)S(1)}, u32[]{:S(2)}) copy-start(f32[256,288]{0,1:T(8,128)S(1)} %fusion.45) | copy-start | bytes 884740
  193.4 174.7 %copy-start.17 = (f32[256,288]{0,1:T(8,128)}, f32[256,288]{0,1:T(8,128)S(1)}, u32[]{:S(2)}) copy-start(f32[256,288]{0,1:T(8,128)S(1)} %fusion.47) | copy-start | bytes 884740
  282.0 89.3 %copy-start.19 = (f32[256,288]{0,1:T(8,128)}, f32[256,288]{0,1:T(8,128)S(1)}, u32[]{:S(2)}) copy-start(f32[256,288]{0,1:T(8,128)S(1)} %fusion.43) | copy-start | bytes 884740
  456.6 3.5 copy-start
  549.0 0.7 copy-start.14
  549.1 310.7 %reduce-scatter.10.cloned.1.call-start = ((), (), s32[]{:S(2)}) async-start(), calls=%async_computation.9 | async-start | bytes 1824768
  719.7 1.3 copy-start.10
  720.9 1.5 copy-start.1
  722.4 1.3 copy-start.3
  722.4 1.3 copy-start.13
  722.4 1.3 copy-start.16
  722.4 1.4 copy-start.18
  722.4 1.5 copy-start.20
  722.4 1.6 copy-start.21
  726.4 265.6 %reduce-scatter.12.cloned.1.call-start = ((), (), s32[]{:S(2)}) async-start(), calls=%async_computation.10 | async-start | bytes 1824768
  729.7 1.3 copy-start.11
  729.8 394.3 %reduce-scatter.14.cloned.1.call-start = ((), (), s32[]{:S(2)}) async-start(), calls=%async_computation.11 | async-start | bytes 1824768
  733.2 126.5 %copy-start.4 = (bf16[72,288]{1,0:T(8,128)(2,1)S(1)}, bf16[72,288]{1,0:T(8,128)(2,1)}, u32[]{:S(2)}) copy-start(bf16[72,288]{1,0:T(8,128)(2,1)} %param.20) | copy-start | bytes 124420
  733.2 126.5 %copy-start.7 = (f32[72,288]{1,0:T(8,128)S(1)}, f32[72,288]{1,0:T(8,128)}, u32[]{:S(2)}) copy-start(f32[72,288]{1,0:T(8,128)} %param.23) | copy-start | bytes 248836
  733.2 258.8 %copy-start.5 = (bf16[72,288]{1,0:T(8,128)(2,1)S(1)}, bf16[72,288]{1,0:T(8,128)(2,1)}, u32[]{:S(2)}) copy-start(bf16[72,288]{1,0:T(8,128)(2,1)} %param.21) | copy-start | bytes 124420
  733.2 258.8 %copy-start.8 = (f32[72,288]{1,0:T(8,128)S(1)}, f32[72,288]{1,0:T(8,128)}, u32[]{:S(2)}) copy-start(f32[72,288]{1,0:T(8,128)} %param.24) | copy-start | bytes 248836
  733.2 390.9 %copy-start.6 = (bf16[288,72]{0,1:T(8,128)(2,1)S(1)}, bf16[288,72]{0,1:T(8,128)(2,1)}, u32[]{:S(2)}) copy-start(bf16[288,72]{0,1:T(8,128)(2,1)} %param.22) | copy-start | bytes 124420
  733.2 390.8 %copy-start.9 = (f32[288,72]{0,1:T(8,128)S(1)}, f32[288,72]{0,1:T(8,128)}, u32[]{:S(2)}) copy-start(f32[288,72]{0,1:T(8,128)} %param.25) | copy-start | bytes 248836
Sparse Core Ops, SparseCore 0:
  11.4 91.1 all-gather.8
  105.9 85.1 all-gather.6
  194.5 85.1 all-gather.10
  282.9 85.1 all-gather.12
  371.4 85.1 all-gather.14
  459.8 85.1 all-gather.16
  549.2 167.9 all-reduce.5
  726.5 133.1 reduce-scatter.9
  864.5 127.4 reduce-scatter.11
  996.6 127.4 reduce-scatter.13
where the time goes:
time: 1140 us; the launch traced here: 1130 us
  waiting for transfers between devices  984 us (86%)
  blocking collectives  91 us (8%)
  matrix products  31.3 us (3%)
  between operations  14.3 us (1%)
    unnamed x13, waiting for transfers between devices  392 us
    psum x1, blocking collectives, per_device(): counts = lax.psum(jnp.sum(onehot, axis=0), 'seq')  91 us
    all_gather x1, waiting for transfers between devices, per_device(): lax.all_gather(dir_gate, 'seq', axis=0, tiled=True)  89.7 us
    all_gather x1, waiting for transfers between devices, per_device(): lax.all_gather(w_up, 'seq', axis=0, tiled=True)  86.3 us
    all_gather x1, waiting for transfers between devices, per_device(): lax.all_gather(dir_up, 'seq', axis=0, tiled=True)  86.1 us
    all_gather x1, waiting for transfers between devices, per_device(): lax.all_gather(w_gate, 'seq', axis=0, tiled=True)  85.9 us
    all_gather x1, waiting for transfers between devices, per_device(): lax.all_gather(w_down, 'seq', axis=1, tiled=True)  85.2 us
    all_gather x1, waiting for transfers between devices, per_device(): lax.all_gather(dir_down, 'seq', axis=1, tiled=True)  82.7 us
  transfers between devices with their start and end apart: 10, of which 10 were waited for; matrix products, arithmetic and copies ran while one was open for 2% of the time, Pallas kernels for 0%

commit v1 on v0

v1 whole, which is shorter than its diff:
```python
import jax
import jax.numpy as jnp
from jax import lax
from jax.sharding import PartitionSpec as P

gelu_rate = 0.7978845608028654
gelu_cubic = 0.044715
beta_decay = 0.9
norm_eps = 1e-06

NZ = 8
ROWS = 72
UNITS = 288
BF = jnp.bfloat16
F32 = jnp.float32


def gelu_parts(pre):
    inner = gelu_rate * (pre + gelu_cubic * pre * pre * pre)
    slope = gelu_rate * (1.0 + 3.0 * gelu_cubic * pre * pre)
    bend = 6.0 * gelu_rate * gelu_cubic * pre
    tanh_val = jnp.tanh(inner)
    sech_sq = 1.0 - tanh_val * tanh_val
    value = 0.5 * pre * (1.0 + tanh_val)
    first = 0.5 * (1.0 + tanh_val) + 0.5 * pre * sech_sq * slope
    second = sech_sq * (slope + 0.5 * pre * (bend - 2.0 * tanh_val * slope * slope))
    return (value, first, second)


def product(left, right):
    return jnp.dot(left, right, preferred_element_type=F32)


def against(left, right):
    return lax.dot_general(left, right, (((1,), (1,)), ((), ())), preferred_element_type=F32)


def over_tokens(left, right):
    return lax.dot_general(left, right, (((0,), (0,)), ((), ())), preferred_element_type=F32)


def blend(ema, probe, hvp):
    return beta_decay * ema + (1.0 - beta_decay) * (probe.astype(F32) * hvp)


def z_shift(array, by):
    perm = [(s, (s // 16) * 16 + ((s // 2 % 8 + by) % 8) * 2 + s % 2) for s in range(32)]
    return lax.ppermute(array, "seq", perm)


def seq_swap(array, bit):
    return lax.ppermute(array, "seq", [(s, s ^ bit) for s in range(32)])


def x_shift(array, by):
    perm = [(t, (t // 4) * 4 + (t % 4 + by) % 4) for t in range(16)]
    return lax.ppermute(array, "tensor", perm)


def y_swap(array, bit):
    return lax.ppermute(array, "tensor", [(t, t ^ (bit * 4)) for t in range(16)])


def half_of(n):
    return 128 * ((n + 255) // 256)


def gather_z(chunk, z):
    r, rows, n = chunk.shape
    h = half_of(n)
    buf = jnp.zeros((r, NZ, rows, n), chunk.dtype)

    def put(buf, piece, at, col=0):
        return lax.dynamic_update_slice(buf, piece[:, None], (0, (z + at) % NZ, 0, col))

    buf = put(buf, chunk, 0)
    up = down = chunk
    for k in (1, 2, 3):
        up = z_shift(up, 1)
        down = z_shift(down, -1)
        buf = put(buf, up, NZ - k)
        buf = put(buf, down, k)
    buf = put(buf, z_shift(up[:, :, :h], 1), 4)
    buf = put(buf, z_shift(down[:, :, h:], -1), 4, h)
    return buf


def scatter_z(parts, z):
    n = parts.shape[-1]
    h = half_of(n)

    def block(at):
        return lax.dynamic_index_in_dim(parts, (z + at) % NZ, 0, keepdims=False)

    def add(left, right):
        return (left.astype(F32) + right.astype(F32)).astype(BF)

    far = block(4)
    up, down = z_shift(far[:, :h], 1), z_shift(far[:, h:], -1)
    ahead, behind = block(3), block(5)
    up = jnp.concatenate([add(ahead[:, :h], up), ahead[:, h:]], axis=1)
    down = jnp.concatenate([behind[:, :h], add(behind[:, h:], down)], axis=1)
    for k in (2, 1):
        up, down = add(block(k), z_shift(up, 1)), add(block(NZ - k), z_shift(down, -1))
    up, down = z_shift(up, 1), z_shift(down, -1)
    return block(0).astype(F32) + up.astype(F32) + down.astype(F32)


def scatter_tensor(part, x, y):
    n = part.shape[1]
    h = n // 2
    part = part.reshape(4, 64, n)

    def block(at):
        return lax.dynamic_index_in_dim(part, (x + at) % 4, 0, keepdims=False)

    def add(left, right):
        return (left.astype(F32) + right.astype(F32)).astype(BF)

    far, ahead, behind = block(2), block(1), block(3)
    up, down = x_shift(far[:, :h], 1), x_shift(far[:, h:], -1)
    up = x_shift(jnp.concatenate([add(ahead[:, :h], up), ahead[:, h:]], axis=1), 1)
    down = x_shift(jnp.concatenate([behind[:, :h], add(behind[:, h:], down)], axis=1), -1)
    total = block(0).astype(F32) + up.astype(F32) + down.astype(F32)
    total = total.reshape(2, 2, 16, n)
    low = y % 2
    mine = lax.dynamic_index_in_dim(total, low, 1, keepdims=False)
    other = lax.dynamic_index_in_dim(total, 1 - low, 1, keepdims=False).astype(BF)
    mine = mine + y_swap(other, 1).astype(F32)
    high = y // 2
    own = lax.dynamic_index_in_dim(mine, high, 0, keepdims=False)
    other = lax.dynamic_index_in_dim(mine, 1 - high, 0, keepdims=False).astype(BF)
    return own + y_swap(other, 2).astype(F32)


def gather_tensor(own, x, y):
    n = own.shape[1]
    h = n // 2
    low, high = y % 2, y // 2
    other = y_swap(own, 2)
    pair = jnp.where(high == 0, jnp.stack([own, other]), jnp.stack([other, own]))
    other = y_swap(pair, 1)
    rows = jnp.where(low == 0, jnp.stack([pair, other], axis=1), jnp.stack([other, pair], axis=1))
    rows = rows.reshape(64, n)
    buf = jnp.zeros((4, 64, n), own.dtype)

    def put(buf, piece, at, col=0):
        return lax.dynamic_update_slice(buf, piece[None], ((x + at) % 4, 0, col))

    buf = put(buf, rows, 0)
    up, down = x_shift(rows, 1), x_shift(rows, -1)
    buf = put(put(buf, up, 3), down, 1)
    buf = put(buf, x_shift(up[:, :h], 1), 2)
    buf = put(buf, x_shift(down[:, h:], -1), 2, h)
    return buf.reshape(256, n)


def relative(rows, y, c):
    m = rows.shape[0]
    parts = rows.reshape(m, 2, NZ, 2, ROWS).transpose(1, 3, 0, 2, 4).reshape(2, 2, m, NZ * ROWS)
    parts = jnp.where(y == 0, parts, parts[::-1])
    parts = jnp.where(c == 0, parts, parts[:, ::-1])
    return parts.transpose(2, 0, 1, 3).reshape(m, 4 * NZ * ROWS)


def per_device(
    tokens,
    target,
    segment_ids,
    norm_gain,
    w_gate,
    w_up,
    w_down,
    dir_gate,
    dir_up,
    dir_down,
    ema_gate,
    ema_up,
    ema_down,
):
    s = lax.axis_index("seq")
    t = lax.axis_index("tensor")
    yh, z, c = s // 16, (s // 2) % 8, s % 2
    yl, x = t // 4, t % 4

    own_in = jnp.concatenate([w_gate, w_up, dir_gate, dir_up], axis=1)[None]
    own_out = jnp.concatenate([w_down.T, dir_down.T], axis=1)[None]
    across_in = seq_swap(own_in, 16)
    across_out = seq_swap(own_out, 16)
    near = gather_z(own_in, z)
    near_other = seq_swap(near, 1)
    away = gather_z(across_in, z)
    away_other = seq_swap(away, 1)
    outs = gather_z(jnp.concatenate([own_out, across_out], axis=0), z)
    outs_other = seq_swap(outs, 1)

    def joined(mine, other):
        return jnp.concatenate([mine[0], other[0]], axis=0).reshape(2 * NZ * ROWS, mine.shape[-1])

    labels = jnp.arange(32, dtype=jnp.int32)
    onehot = (segment_ids[:, None] == labels[None, :]).astype(F32)
    counts = jnp.sum(onehot, axis=0, keepdims=True)
    for bit in (1, 2, 4, 8, 16):
        counts = counts + seq_swap(counts, bit)

    wide = tokens.astype(F32)
    scale = lax.rsqrt(jnp.mean(wide * wide, axis=1, keepdims=True) + norm_eps)
    normed = (wide * scale * norm_gain).astype(BF)
    normed = relative(normed, yh, c)

    half = 2 * NZ * ROWS
    pre = product(normed[:, :half], joined(near, near_other)) + product(
        normed[:, half:], joined(away, away_other)
    )
    gate, upper, gate_dot, upper_dot = (pre[:, i * UNITS : (i + 1) * UNITS] for i in range(4))
    value, first, second = gelu_parts(gate)
    hidden = (value * upper).astype(BF)
    hidden_dot = (first * gate_dot * upper + value * upper_dot).astype(BF)

    down_all = jnp.stack([outs, outs_other], axis=1).reshape(4 * NZ * ROWS, 2 * UNITS)
    mixed_part = against(hidden, down_all[:, :UNITS]).astype(BF)
    mixed_dot_part = against(jnp.concatenate([hidden_dot, hidden], axis=1), down_all).astype(BF)

    mixed = scatter_tensor(mixed_part, x, yl)
    mixed_dot = scatter_tensor(mixed_dot_part, x, yl)

    at = x * 64 + yl * 16
    my_tokens = relative(lax.dynamic_slice_in_dim(tokens, at, 16, 0), yh, c).astype(F32)
    my_target = relative(lax.dynamic_slice_in_dim(target, at, 16, 0), yh, c).astype(F32)
    my_hot = lax.dynamic_slice_in_dim(onehot, at, 16, 0)
    lengths = jnp.sum(my_hot * counts, axis=1, keepdims=True)
    my_grad = ((my_tokens + mixed - my_target) / lengths).astype(BF)
    my_grad_dot = (mixed_dot / lengths).astype(BF)
    grad_out = gather_tensor(my_grad, x, yl)
    grad_out_dot = gather_tensor(my_grad_dot, x, yl)

    back = product(grad_out, down_all)
    back_dot = product(grad_out_dot, down_all[:, :UNITS])
    grad_hidden = back[:, :UNITS]
    grad_hidden_dot = back_dot + back[:, UNITS:]
    grad_gate_dot = (
        (grad_hidden_dot * upper + grad_hidden * upper_dot) * first
        + grad_hidden * upper * second * gate_dot
    ).astype(BF)
    grad_upper_dot = (grad_hidden_dot * value + grad_hidden * first * gate_dot).astype(BF)
    grads = jnp.concatenate([grad_gate_dot, grad_upper_dot], axis=1)

    def terms(lo):
        part_in = over_tokens(normed[:, lo : lo + half], grads).astype(BF)
        part_out = (
            over_tokens(grad_out[:, lo : lo + half], hidden_dot)
            + over_tokens(grad_out_dot[:, lo : lo + half], hidden)
        ).astype(BF)
        part = jnp.concatenate([part_in, part_out], axis=1).reshape(2, NZ, ROWS, 3 * UNITS)
        return (part[0].astype(F32) + seq_swap(part[1], 1).astype(F32)).astype(BF)

    far_sum = scatter_z(terms(half), z)
    far_sum = seq_swap(far_sum.astype(BF), 16).astype(F32)
    hvp = scatter_z(terms(0), z) + far_sum
    return (
        blend(ema_gate, dir_gate, hvp[:, :UNITS]),
        blend(ema_up, dir_up, hvp[:, UNITS : 2 * UNITS]),
        blend(ema_down, dir_down, hvp[:, 2 * UNITS :].T),
    )


def solution(mesh):
    in_specs = (
        P("seq", None),
        P("seq", None),
        P("seq"),
        P(),
        P("seq", "tensor"),
        P("seq", "tensor"),
        P("tensor", "seq"),
        P("seq", "tensor"),
        P("seq", "tensor"),
        P("tensor", "seq"),
        P("seq", "tensor"),
        P("seq", "tensor"),
        P("tensor", "seq"),
    )
    out_specs = (P("seq", "tensor"), P("seq", "tensor"), P("tensor", "seq"))
    return jax.shard_map(
        per_device, mesh=mesh, in_specs=in_specs, out_specs=out_specs, check_vma=False
    )
```

time: 1140 us -> 367 us (0.32)
  waiting for transfers between devices: 984 us -> 45.7 us
  starting transfers between devices: 0.39 us -> 264 us
  blocking collectives: 91 us -> 0 us
  matrix products: 31.3 us -> 10.9 us
  local copies, waits for them, and re-layouts: 2.98 us -> 20 us
    all_gather x6 -> x0, waiting for transfers between devices: 516 us -> none  [the longest x1 89.7 us: per_device(): lax.all_gather(dir_gate, 'seq', axis=0, tiled=True)]
    unnamed x13 -> x0, waiting for transfers between devices: 392 us -> none
    ppermute x0 -> x77, starting transfers between devices: none -> 264 us  [the longest x40 140 us: z_shift(): return lax.ppermute(array, 'seq', perm)]
    psum x1 -> x0, blocking collectives: 91 us -> none  [per_device(): counts = lax.psum(jnp.sum(onehot, axis=0), 'seq')]
    psum x1 -> x0, waiting for transfers between devices: 76.2 us -> none  [per_device(): lax.psum(mixed_part.astype(jnp.bfloat16), 'tensor').astype(jnp.float32)]
    ppermute x0 -> x77, waiting for transfers between devices: none -> 45.7 us  [the longest x13 24.3 us: seq_swap(): return lax.ppermute(array, 'seq', [(s, s ^ bit) for s in range(32)])]
    dot_general x8 -> x4, matrix products: 20.3 us -> 5.67 us  [product(): return jnp.dot(left, right, preferred_element_type=F32)]
  transfers between devices with their start and end apart: 10 -> 77, of which waited for: 10 -> 20; matrix products, arithmetic and copies ran while one was open for 2% -> 9% of each run, Pallas kernels for 0% -> 0%
where the time goes in v1:
time: 367 us; the launch traced here: 363 us
  starting transfers between devices  264 us (72%)
  waiting for transfers between devices  45.7 us (12%)
  local copies, waits for them, and re-layouts  20 us (5%)
  other arithmetic  19.4 us (5%)
  matrix products  10.9 us (3%)
    ppermute x40, starting transfers between devices, z_shift(): return lax.ppermute(array, 'seq', perm)  140 us
    ppermute x16, starting transfers between devices, x_shift(): return lax.ppermute(array, 'tensor', perm)  57.2 us
    ppermute x13, starting transfers between devices, seq_swap(): return lax.ppermute(array, 'seq', [(s, s ^ bit) for s in range(32)])  39.8 us
    ppermute x8, starting transfers between devices, y_swap(): return lax.ppermute(array, 'tensor', [(t, t ^ bit * 4) for t in range(16)])  27.2 us
    ppermute x13, waiting for transfers between devices, seq_swap(): return lax.ppermute(array, 'seq', [(s, s ^ bit) for s in range(32)])  24.3 us
    ppermute x40, waiting for transfers between devices, z_shift(): return lax.ppermute(array, 'seq', perm)  11.8 us
    dynamic_update_slice x26, local copies, waits for them, and re-layouts, put(): lax.dynamic_update_slice(buf, piece[:, None], (0, (z + at) % NZ, 0, col))  9.3 us
  transfers between devices with their start and end apart: 77, of which 20 were waited for; matrix products, arithmetic and copies ran while one was open for 9% of the time, Pallas kernels for 0%

profile of v1, /device:TPU:56, one launch (start us, length us, event | category | flops | bytes accessed | tf_op | source)
XLA Modules:
  0.0 363.4 jit_solution(13326620814105901156)
XLA Ops:
  1.8 4.3 %collective-permute-start = (bf16[1,72,1152]{2,1,0:T(8,128)(2,1)S(1)}, bf16[1,72,1152]{2,1,0:T(8,128)(2,1)}, u32[]{:S(2)}, u32[]{:S(2)}) collective-permute-start(bf16[1,72,1152]{2,1,0:T(8,128)(2,1)S(1)} %bitcast.308), channel_id=1, source_target_pairs={{0,32},{16,48},{32,64},{48,80},{64,96},{80,112},{96,128},{112,144}... | collective-permute-start | bytes 497672 | tf_op jit(solution)/shard_map/ppermute | solution.py:48
  6.1 8.6 %collective-permute-start.1 = (bf16[1,72,1152]{2,1,0:T(8,128)(2,1)S(1)}, bf16[1,72,1152]{2,1,0:T(8,128)(2,1)}, u32[]{:S(2)}, u32[]{:S(2)}) collective-permute-start(bf16[1,72,1152]{2,1,0:T(8,128)(2,1)S(1)} %bitcast.309), channel_id=1, source_target_pairs={{0,224},{16,240},{32,0},{48,16},{64,32},{80,48},{96,64},{112,80},{... | collective-permute-start | bytes 497672 | tf_op jit(solution)/shard_map/ppermute | solution.py:48
  14.7 4.7 %collective-permute-start.9 = (bf16[1,72,1152]{2,1,0:T(8,128)(2,1)S(1)}, bf16[1,72,1152]{2,1,0:T(8,128)(2,1)}, u32[]{:S(2)}, u32[]{:S(2)}) collective-permute-start(bf16[1,72,1152]{2,1,0:T(8,128)(2,1)S(1)} %bitcast.310), channel_id=1, source_target_pairs={{0,256},{16,272},{32,288},{48,304},{64,320},{80,336},{96,352},{112... | collective-permute-start | bytes 497672 | tf_op jit(solution)/shard_map/ppermute | solution.py:52
  20.3 5.0 %collective-permute-start.19 = (bf16[1,72,576]{2,1,0:T(8,128)(2,1)S(1)}, bf16[1,72,576]{2,1,0:T(8,128)(2,1)S(1)}, u32[]{:S(2)}, u32[]{:S(2)}) collective-permute-start(bf16[1,72,576]{2,1,0:T(8,128)(2,1)S(1)} %maximum_bitcast_fusion.2), channel_id=1, source_target_pairs={{0,256},{16,272},{32,288},{48,304},{64,320},{80,336},{96,352},{112... | collective-permute-start | bytes 248840 | tf_op jit(solution)/shard_map/ppermute | solution.py:52
  34.2 1.9 collective-permute-start.20
  36.3 5.1 %collective-permute-start.21 = (bf16[2,72,576]{2,1,0:T(8,128)(2,1)S(1)}, bf16[2,72,576]{2,1,0:T(8,128)(2,1)S(1)}, u32[]{:S(2)}, u32[]{:S(2)}) collective-permute-start(bf16[2,72,576]{2,1,0:T(8,128)(2,1)S(1)} %pad_maximum_fusion.10), channel_id=1, source_target_pairs={{0,224},{16,240},{32,0},{48,16},{64,32},{80,48},{96,64},{112,80},{... | collective-permute-start | bytes 497672 | tf_op jit(solution)/shard_map/ppermute | solution.py:48
  45.2 5.1 %collective-permute-start.3 = (bf16[1,72,1152]{2,1,0:T(8,128)(2,1)}, bf16[1,72,1152]{2,1,0:T(8,128)(2,1)S(1)}, u32[]{:S(2)}, u32[]{:S(2)}) collective-permute-start(bf16[1,72,1152]{2,1,0:T(8,128)(2,1)} %collective-permute-done.1), channel_id=1, source_target_pairs={{0,224},{16,240},{32,0},{48,16},{64,32},{80,48},{96,64},{112,80},{... | collective-permute-start | bytes 497672 | tf_op jit(solution)/shard_map/ppermute | solution.py:48
  55.1 5.1 %collective-permute-start.11 = (bf16[1,72,1152]{2,1,0:T(8,128)(2,1)}, bf16[1,72,1152]{2,1,0:T(8,128)(2,1)S(1)}, u32[]{:S(2)}, u32[]{:S(2)}) collective-permute-start(bf16[1,72,1152]{2,1,0:T(8,128)(2,1)} %collective-permute-done.9), channel_id=1, source_target_pairs={{0,224},{16,240},{32,0},{48,16},{64,32},{80,48},{96,64},{112,80},{... | collective-permute-start | bytes 497672 | tf_op jit(solution)/shard_map/ppermute | solution.py:48
  64.6 5.1 %collective-permute-start.23 = (bf16[2,72,576]{2,1,0:T(8,128)(2,1)S(1)}, bf16[2,72,576]{2,1,0:T(8,128)(2,1)S(1)}, u32[]{:S(2)}, u32[]{:S(2)}) collective-permute-start(bf16[2,72,576]{2,1,0:T(8,128)(2,1)S(1)} %collective-permute-done.21), channel_id=1, source_target_pairs={{0,224},{16,240},{32,0},{48,16},{64,32},{80,48},{96,64},{112,80},{... | collective-permute-start | bytes 497672 | tf_op jit(solution)/shard_map/ppermute | solution.py:48
  71.8 5.1 %collective-permute-start.5 = (bf16[1,72,1152]{2,1,0:T(8,128)(2,1)S(1)}, bf16[1,72,1152]{2,1,0:T(8,128)(2,1)S(1)}, u32[]{:S(2)}, u32[]{:S(2)}) collective-permute-start(bf16[1,72,1152]{2,1,0:T(8,128)(2,1)S(1)} %collective-permute-done.3), channel_id=1, source_target_pairs={{0,224},{16,240},{32,0},{48,16},{64,32},{80,48},{96,64},{112,80},{... | collective-permute-start | bytes 497672 | tf_op jit(solution)/shard_map/ppermute | solution.py:48
  79.6 5.1 %collective-permute-start.13 = (bf16[1,72,1152]{2,1,0:T(8,128)(2,1)S(1)}, bf16[1,72,1152]{2,1,0:T(8,128)(2,1)S(1)}, u32[]{:S(2)}, u32[]{:S(2)}) collective-permute-start(bf16[1,72,1152]{2,1,0:T(8,128)(2,1)S(1)} %collective-permute-done.11), channel_id=1, source_target_pairs={{0,224},{16,240},{32,0},{48,16},{64,32},{80,48},{96,64},{112,80},{... | collective-permute-start | bytes 497672 | tf_op jit(solution)/shard_map/ppermute | solution.py:48
  88.7 5.1 %collective-permute-start.25 = (bf16[2,72,576]{2,1,0:T(8,128)(2,1)S(1)}, bf16[2,72,576]{2,1,0:T(8,128)(2,1)S(1)}, u32[]{:S(2)}, u32[]{:S(2)}) collective-permute-start(bf16[2,72,576]{2,1,0:T(8,128)(2,1)S(1)} %collective-permute-done.23), channel_id=1, source_target_pairs={{0,224},{16,240},{32,0},{48,16},{64,32},{80,48},{96,64},{112,80},{... | collective-permute-start | bytes 497672 | tf_op jit(solution)/shard_map/ppermute | solution.py:48
  95.8 5.1 %collective-permute-start.7 = (bf16[1,72,512]{2,1,0:T(8,128)(2,1)S(1)}, bf16[1,72,512]{2,1,0:T(8,128)(2,1)S(1)}, u32[]{:S(2)}, u32[]{:S(2)}) collective-permute-start(bf16[1,72,512]{2,1,0:T(8,128)(2,1)S(1)} %slice.225), channel_id=1, source_target_pairs={{0,224},{16,240},{32,0},{48,16},{64,32},{80,48},{96,64},{112,80},{... | collective-permute-start | bytes 221192 | tf_op jit(solution)/shard_map/ppermute | solution.py:48
  103.6 5.1 %collective-permute-start.15 = (bf16[1,72,1152]{2,1,0:T(8,128)(2,1)S(1)}, bf16[1,72,1152]{2,1,0:T(8,128)(2,1)S(1)}, u32[]{:S(2)}, u32[]{:S(2)}) collective-permute-start(bf16[1,72,1152]{2,1,0:T(8,128)(2,1)S(1)} %collective-permute-done.13), channel_id=1, source_target_pairs={{0,224},{16,240},{32,0},{48,16},{64,32},{80,48},{96,64},{112,80},{... | collective-permute-start | bytes 497672 | tf_op jit(solution)/shard_map/ppermute | solution.py:48
  110.8 5.1 %collective-permute-start.27 = (bf16[2,72,192]{2,1,0:T(8,128)(2,1)S(1)}, bf16[2,72,192]{2,1,0:T(8,128)(2,1)S(1)}, u32[]{:S(2)}, u32[]{:S(2)}) collective-permute-start(bf16[2,72,192]{2,1,0:T(8,128)(2,1)S(1)} %slice.234), channel_id=1, source_target_pairs={{0,224},{16,240},{32,0},{48,16},{64,32},{80,48},{96,64},{112,80},{... | collective-permute-start | bytes 165896 | tf_op jit(solution)/shard_map/ppermute | solution.py:48
  116.0 1.9 collective-permute-start.8
  121.2 5.1 %collective-permute-start.17 = (bf16[1,72,512]{2,1,0:T(8,128)(2,1)S(1)}, bf16[1,72,512]{2,1,0:T(8,128)(2,1)S(1)}, u32[]{:S(2)}, u32[]{:S(2)}) collective-permute-start(bf16[1,72,512]{2,1,0:T(8,128)(2,1)S(1)} %slice.228), channel_id=1, source_target_pairs={{0,224},{16,240},{32,0},{48,16},{64,32},{80,48},{96,64},{112,80},{... | collective-permute-start | bytes 221192 | tf_op jit(solution)/shard_map/ppermute | solution.py:48
  126.5 1.9 collective-permute-start.28
  129.7 2.4 collective-permute-start.18
  133.2 3.0 reverse_select_fusion
  139.0 3.5 collective-permute-done.36
  142.5 3.4 collective-permute-start.37
  146.0 2.9 collective-permute-done.37
  148.9 5.1 %collective-permute-start.38 = (f32[1,32]{1,0:T(1,128)S(1)}, f32[1,32]{1,0:T(1,128)S(1)}, u32[]{:S(2)}, u32[]{:S(2)}) collective-permute-start(f32[1,32]{1,0:T(1,128)S(1)} %add.523), channel_id=1, source_target_pairs={{0,128},{16,144},{32,160},{48,176},{64,192},{80,208},{96,224},{112... | collective-permute-start | bytes 392 | tf_op jit(solution)/shard_map/ppermute | solution.py:52
  154.0 4.2 %collective-permute-done.38 = f32[1,32]{1,0:T(1,128)S(1)} collective-permute-done((f32[1,32]{1,0:T(1,128)S(1)}, f32[1,32]{1,0:T(1,128)S(1)}, u32[]{:S(2)}, u32[]{:S(2)}) %collective-permute-start.38) | collective-permute-done | bytes 160 | tf_op jit(solution)/shard_map/ppermute | solution.py:52
  158.2 4.9 %collective-permute-start.39 = (f32[1,32]{1,0:T(1,128)S(1)}, f32[1,32]{1,0:T(1,128)S(1)}, u32[]{:S(2)}, u32[]{:S(2)}) collective-permute-start(f32[1,32]{1,0:T(1,128)S(1)} %add.524), channel_id=1, source_target_pairs={{0,256},{16,272},{32,288},{48,304},{64,320},{80,336},{96,352},{112... | collective-permute-start | bytes 392 | tf_op jit(solution)/shard_map/ppermute | solution.py:52
  163.1 4.4 %collective-permute-done.39 = f32[1,32]{1,0:T(1,128)S(1)} collective-permute-done((f32[1,32]{1,0:T(1,128)S(1)}, f32[1,32]{1,0:T(1,128)S(1)}, u32[]{:S(2)}, u32[]{:S(2)}) %collective-permute-start.39) | collective-permute-done | bytes 160 | tf_op jit(solution)/shard_map/ppermute | solution.py:52
  171.1 2.1 pad_maximum_fusion.2
  178.8 3.4 collective-permute-start.29
  182.2 3.6 %collective-permute-start.31 = (bf16[64,1152]{1,0:T(8,128)(2,1)S(1)}, bf16[64,1152]{1,0:T(8,128)(2,1)S(1)}, u32[]{:S(2)}, u32[]{:S(2)}) collective-permute-start(bf16[64,1152]{1,0:T(8,128)(2,1)S(1)} %get-tuple-element.30), channel_id=1, source_target_pairs={{0,3},{1,0},{2,1},{3,2},{4,7},{5,4},{6,5},{7,6},{8,11},{9,8},{10,9... | collective-permute-start | bytes 442376 | tf_op jit(solution)/shard_map/ppermute | solution.py:57
  186.0 2.2 collective-permute-start.46
  188.2 4.9 %collective-permute-start.48 = (bf16[64,1152]{1,0:T(8,128)(2,1)S(1)}, bf16[64,1152]{1,0:T(8,128)(2,1)S(1)}, u32[]{:S(2)}, u32[]{:S(2)}) collective-permute-start(bf16[64,1152]{1,0:T(8,128)(2,1)S(1)} %get-tuple-element.28), channel_id=1, source_target_pairs={{0,3},{1,0},{2,1},{3,2},{4,7},{5,4},{6,5},{7,6},{8,11},{9,8},{10,9... | collective-permute-start | bytes 442376 | tf_op jit(solution)/shard_map/ppermute | solution.py:57
  195.2 5.1 %collective-permute-start.32 = (bf16[64,2304]{1,0:T(8,128)(2,1)S(1)}, bf16[64,2304]{1,0:T(8,128)(2,1)S(1)}, u32[]{:S(2)}, u32[]{:S(2)}) collective-permute-start(bf16[64,2304]{1,0:T(8,128)(2,1)S(1)} %pad_maximum_fusion.7), channel_id=1, source_target_pairs={{0,3},{1,0},{2,1},{3,2},{4,7},{5,4},{6,5},{7,6},{8,11},{9,8},{10,9... | collective-permute-start | bytes 884744 | tf_op jit(solution)/shard_map/ppermute | solution.py:57
  202.5 5.1 %collective-permute-start.49 = (bf16[64,2304]{1,0:T(8,128)(2,1)S(1)}, bf16[64,2304]{1,0:T(8,128)(2,1)S(1)}, u32[]{:S(2)}, u32[]{:S(2)}) collective-permute-start(bf16[64,2304]{1,0:T(8,128)(2,1)S(1)} %pad_maximum_fusion.9), channel_id=1, source_target_pairs={{0,3},{1,0},{2,1},{3,2},{4,7},{5,4},{6,5},{7,6},{8,11},{9,8},{10,9... | collective-permute-start | bytes 884744 | tf_op jit(solution)/shard_map/ppermute | solution.py:57
  207.8 3.3 collective-permute-start.33
  212.0 3.4 collective-permute-start.50
  215.5 4.5 %collective-permute-start.34 = (bf16[16,2304]{1,0:T(8,128)(2,1)S(1)}, bf16[16,2304]{1,0:T(8,128)(2,1)S(1)}, u32[]{:S(2)}, u32[]{:S(2)}) collective-permute-start(bf16[16,2304]{1,0:T(8,128)(2,1)S(1)} %fusion.71), channel_id=1, source_target_pairs={{0,8},{1,9},{2,10},{3,11},{4,12},{5,13},{6,14},{7,15},{8,0},{9,1},... | collective-permute-start | bytes 221192 | tf_op jit(solution)/shard_map/ppermute | solution.py:61
  220.1 3.4 collective-permute-start.51
  223.6 5.8 %collective-permute-done.51 = bf16[16,2304]{1,0:T(8,128)(2,1)S(1)} collective-permute-done((bf16[16,2304]{1,0:T(8,128)(2,1)S(1)}, bf16[16,2304]{1,0:T(8,128)(2,1)S(1)}, u32[]{:S(2)}, u32[]{:S(2)}) %collective-permute-start.51) | collective-permute-done | bytes 73760 | tf_op jit(solution)/shard_map/ppermute | solution.py:61
  229.5 2.1 collective-permute-start.52
  231.6 4.7 %collective-permute-start.40 = (bf16[16,2304]{1,0:T(8,128)(2,1)S(1)}, bf16[16,2304]{1,0:T(8,128)(2,1)S(1)}, u32[]{:S(2)}, u32[]{:S(2)}) collective-permute-start(bf16[16,2304]{1,0:T(8,128)(2,1)S(1)} %get-tuple-element.34), channel_id=1, source_target_pairs={{0,8},{1,9},{2,10},{3,11},{4,12},{5,13},{6,14},{7,15},{8,0},{9,1},... | collective-permute-start | bytes 221192 | tf_op jit(solution)/shard_map/ppermute | solution.py:61
  239.8 3.9 %collective-permute-start.41 = (bf16[2,16,2304]{2,1,0:T(8,128)(2,1)S(1)}, bf16[2,16,2304]{2,1,0:T(8,128)(2,1)S(1)}, u32[]{:S(2)}, u32[]{:S(2)}) collective-permute-start(bf16[2,16,2304]{2,1,0:T(8,128)(2,1)S(1)} %maximum_select_fusion.3), channel_id=1, source_target_pairs={{0,4},{1,5},{2,6},{3,7},{4,0},{5,1},{6,2},{7,3},{8,12},{9,13},{10,... | collective-permute-start | bytes 442376 | tf_op jit(solution)/shard_map/ppermute | solution.py:61
  246.9 5.7 %collective-permute-start.55 = (bf16[64,2304]{1,0:T(8,128)(2,1)S(1)}, bf16[64,2304]{1,0:T(8,128)(2,1)S(1)}, u32[]{:S(2)}, u32[]{:S(2)}) collective-permute-start(bf16[64,2304]{1,0:T(8,128)(2,1)S(1)} %bitcast.301), channel_id=1, source_target_pairs={{0,3},{1,0},{2,1},{3,2},{4,7},{5,4},{6,5},{7,6},{8,11},{9,8},{10,9... | collective-permute-start | bytes 884744 | tf_op jit(solution)/shard_map/ppermute | solution.py:57
  254.5 5.1 %collective-permute-start.43 = (bf16[64,2304]{1,0:T(8,128)(2,1)S(1)}, bf16[64,2304]{1,0:T(8,128)(2,1)S(1)}, u32[]{:S(2)}, u32[]{:S(2)}) collective-permute-start(bf16[64,2304]{1,0:T(8,128)(2,1)S(1)} %bitcast.304), channel_id=1, source_target_pairs={{0,3},{1,0},{2,1},{3,2},{4,7},{5,4},{6,5},{7,6},{8,11},{9,8},{10,9... | collective-permute-start | bytes 884744 | tf_op jit(solution)/shard_map/ppermute | solution.py:57
  261.9 5.1 %collective-permute-start.57 = (bf16[64,1152]{1,0:T(8,128)(2,1)S(1)}, bf16[64,1152]{1,0:T(8,128)(2,1)S(1)}, u32[]{:S(2)}, u32[]{:S(2)}) collective-permute-start(bf16[64,1152]{1,0:T(8,128)(2,1)S(1)} %slice.251), channel_id=1, source_target_pairs={{0,3},{1,0},{2,1},{3,2},{4,7},{5,4},{6,5},{7,6},{8,11},{9,8},{10,9... | collective-permute-start | bytes 442376 | tf_op jit(solution)/shard_map/ppermute | solution.py:57
  269.0 5.4 %collective-permute-start.45 = (bf16[64,1152]{1,0:T(8,128)(2,1)S(1)}, bf16[64,1152]{1,0:T(8,128)(2,1)S(1)}, u32[]{:S(2)}, u32[]{:S(2)}) collective-permute-start(bf16[64,1152]{1,0:T(8,128)(2,1)S(1)} %slice.242), channel_id=1, source_target_pairs={{0,3},{1,0},{2,1},{3,2},{4,7},{5,4},{6,5},{7,6},{8,11},{9,8},{10,9... | collective-permute-start | bytes 442376 | tf_op jit(solution)/shard_map/ppermute | solution.py:57
  279.1 2.5 fusion.39
  287.6 2.4 collective-permute-start.67
  290.3 2.0 collective-permute-done.67
  292.7 4.6 %collective-permute-start.63 = (bf16[72,352]{1,0:T(8,128)(2,1)S(1)}, bf16[72,352]{1,0:T(8,128)(2,1)S(1)}, u32[]{:S(2)}, u32[]{:S(2)}) collective-permute-start(bf16[72,352]{1,0:T(8,128)(2,1)S(1)} %slice.263), channel_id=1, source_target_pairs={{0,224},{16,240},{32,0},{48,16},{64,32},{80,48},{96,64},{112,80},{... | collective-permute-start | bytes 152072 | tf_op jit(solution)/shard_map/ppermute | solution.py:48
  299.3 5.1 %collective-permute-start.72 = (bf16[72,352]{1,0:T(8,128)(2,1)S(1)}, bf16[72,352]{1,0:T(8,128)(2,1)S(1)}, u32[]{:S(2)}, u32[]{:S(2)}) collective-permute-start(bf16[72,352]{1,0:T(8,128)(2,1)S(1)} %slice.273), channel_id=1, source_target_pairs={{0,224},{16,240},{32,0},{48,16},{64,32},{80,48},{96,64},{112,80},{... | collective-permute-start | bytes 152072 | tf_op jit(solution)/shard_map/ppermute | solution.py:48
  306.5 5.1 %collective-permute-start.64 = (bf16[72,864]{1,0:T(8,128)(2,1)S(1)}, bf16[72,864]{1,0:T(8,128)(2,1)S(1)}, u32[]{:S(2)}, u32[]{:S(2)}) collective-permute-start(bf16[72,864]{1,0:T(8,128)(2,1)S(1)} %pad_maximum_fusion.14), channel_id=1, source_target_pairs={{0,224},{16,240},{32,0},{48,16},{64,32},{80,48},{96,64},{112,80},{... | collective-permute-start | bytes 373256 | tf_op jit(solution)/shard_map/ppermute | solution.py:48
  313.7 3.9 %collective-permute-start.69 = (bf16[72,864]{1,0:T(8,128)(2,1)S(1)}, bf16[72,864]{1,0:T(8,128)(2,1)S(1)}, u32[]{:S(2)}, u32[]{:S(2)}) collective-permute-start(bf16[72,864]{1,0:T(8,128)(2,1)S(1)} %pad_maximum_fusion.15), channel_id=1, source_target_pairs={{0,32},{16,48},{32,64},{48,80},{64,96},{80,112},{96,128},{112,144}... | collective-permute-start | bytes 373256 | tf_op jit(solution)/shard_map/ppermute | solution.py:48
  319.6 2.1 collective-permute-done.69
  321.7 3.8 %collective-permute-start.70 = (bf16[72,864]{1,0:T(8,128)(2,1)S(1)}, bf16[72,864]{1,0:T(8,128)(2,1)S(1)}, u32[]{:S(2)}, u32[]{:S(2)}) collective-permute-start(bf16[72,864]{1,0:T(8,128)(2,1)S(1)} %fusion.45), channel_id=1, source_target_pairs={{0,32},{16,48},{32,64},{48,80},{64,96},{80,112},{96,128},{112,144}... | collective-permute-start | bytes 373256 | tf_op jit(solution)/shard_map/ppermute | solution.py:48
  328.1 2.8 collective-permute-done.70
  331.0 2.5 collective-permute-start.74
  334.4 2.1 collective-permute-start.65
  336.5 3.8 %collective-permute-start.62 = (bf16[72,864]{1,0:T(8,128)(2,1)S(1)}, bf16[72,864]{1,0:T(8,128)(2,1)S(1)}, u32[]{:S(2)}, u32[]{:S(2)}) collective-permute-start(bf16[72,864]{1,0:T(8,128)(2,1)S(1)} %get-tuple-element.17), channel_id=1, source_target_pairs={{0,32},{16,48},{32,64},{48,80},{64,96},{80,112},{96,128},{112,144}... | collective-permute-start | bytes 373256 | tf_op jit(solution)/shard_map/ppermute | solution.py:48
  340.4 2.8 collective-permute-start.71
  343.2 4.4 %collective-permute-start.75 = (bf16[72,864]{1,0:T(8,128)(2,1)S(1)}, bf16[72,864]{1,0:T(8,128)(2,1)S(1)}, u32[]{:S(2)}, u32[]{:S(2)}) collective-permute-start(bf16[72,864]{1,0:T(8,128)(2,1)S(1)} %fusion.44), channel_id=1, source_target_pairs={{0,224},{16,240},{32,0},{48,16},{64,32},{80,48},{96,64},{112,80},{... | collective-permute-start | bytes 373256 | tf_op jit(solution)/shard_map/ppermute | solution.py:48
  347.7 2.0 collective-permute-start.66
  350.6 2.3 collective-permute-start.76
  354.5 7.3 %collective-permute-done.76 = bf16[72,864]{1,0:T(8,128)(2,1)S(1)} collective-permute-done((bf16[72,864]{1,0:T(8,128)(2,1)S(1)}, bf16[72,864]{1,0:T(8,128)(2,1)S(1)}, u32[]{:S(2)}, u32[]{:S(2)}) %collective-permute-start.76) | collective-permute-done | bytes 124448 | tf_op jit(solution)/shard_map/ppermute | solution.py:52
  (290 shorter events, 101.3 us)
Async XLA Ops:
  1.8 34.5 %collective-permute-start = (bf16[1,72,1152]{2,1,0:T(8,128)(2,1)S(1)}, bf16[1,72,1152]{2,1,0:T(8,128)(2,1)}, u32[]{:S(2)}, u32[]{:S(2)}) collective-permute-start(bf16[1,72,1152]{2,1,0:T(8,128)(2,1)S(1)} %bitcast.308), channel_id=1, source_target_pairs={{0,32},{16,48},{32,64},{48,80},{64,96},{80,112},{96,128},{112,144}... | collective-permute-start | bytes 497672 | tf_op jit(solution)/shard_map/ppermute | solution.py:48
  6.1 36.3 %collective-permute-start.1 = (bf16[1,72,1152]{2,1,0:T(8,128)(2,1)S(1)}, bf16[1,72,1152]{2,1,0:T(8,128)(2,1)}, u32[]{:S(2)}, u32[]{:S(2)}) collective-permute-start(bf16[1,72,1152]{2,1,0:T(8,128)(2,1)S(1)} %bitcast.309), channel_id=1, source_target_pairs={{0,224},{16,240},{32,0},{48,16},{64,32},{80,48},{96,64},{112,80},{... | collective-permute-start | bytes 497672 | tf_op jit(solution)/shard_map/ppermute | solution.py:48
  14.7 30.5 %collective-permute-start.9 = (bf16[1,72,1152]{2,1,0:T(8,128)(2,1)S(1)}, bf16[1,72,1152]{2,1,0:T(8,128)(2,1)}, u32[]{:S(2)}, u32[]{:S(2)}) collective-permute-start(bf16[1,72,1152]{2,1,0:T(8,128)(2,1)S(1)} %bitcast.310), channel_id=1, source_target_pairs={{0,256},{16,272},{32,288},{48,304},{64,320},{80,336},{96,352},{112... | collective-permute-start | bytes 497672 | tf_op jit(solution)/shard_map/ppermute | solution.py:52
  20.3 13.8 %collective-permute-start.19 = (bf16[1,72,576]{2,1,0:T(8,128)(2,1)S(1)}, bf16[1,72,576]{2,1,0:T(8,128)(2,1)S(1)}, u32[]{:S(2)}, u32[]{:S(2)}) collective-permute-start(bf16[1,72,576]{2,1,0:T(8,128)(2,1)S(1)} %maximum_bitcast_fusion.2), channel_id=1, source_target_pairs={{0,256},{16,272},{32,288},{48,304},{64,320},{80,336},{96,352},{112... | collective-permute-start | bytes 248840 | tf_op jit(solution)/shard_map/ppermute | solution.py:52
  26.2 110.9 %collective-permute-start.35 = (f32[1,32]{1,0:T(1,128)S(1)}, f32[1,32]{1,0:T(1,128)S(1)}, u32[]{:S(2)}, u32[]{:S(2)}) collective-permute-start(f32[1,32]{1,0:T(1,128)S(1)} %bitcast.323), channel_id=1, source_target_pairs={{0,16},{16,0},{32,48},{48,32},{64,80},{80,64},{96,112},{112,96},{1... | collective-permute-start | bytes 392 | tf_op jit(solution)/shard_map/ppermute | solution.py:52
  34.2 19.0 %collective-permute-start.20 = (bf16[2,72,576]{2,1,0:T(8,128)(2,1)S(1)}, bf16[2,72,576]{2,1,0:T(8,128)(2,1)S(1)}, u32[]{:S(2)}, u32[]{:S(2)}) collective-permute-start(bf16[2,72,576]{2,1,0:T(8,128)(2,1)S(1)} %pad_maximum_fusion.10), channel_id=1, source_target_pairs={{0,32},{16,48},{32,64},{48,80},{64,96},{80,112},{96,128},{112,144}... | collective-permute-start | bytes 497672 | tf_op jit(solution)/shard_map/ppermute | solution.py:48
  36.3 18.9 %collective-permute-start.21 = (bf16[2,72,576]{2,1,0:T(8,128)(2,1)S(1)}, bf16[2,72,576]{2,1,0:T(8,128)(2,1)S(1)}, u32[]{:S(2)}, u32[]{:S(2)}) collective-permute-start(bf16[2,72,576]{2,1,0:T(8,128)(2,1)S(1)} %pad_maximum_fusion.10), channel_id=1, source_target_pairs={{0,224},{16,240},{32,0},{48,16},{64,32},{80,48},{96,64},{112,80},{... | collective-permute-start | bytes 497672 | tf_op jit(solution)/shard_map/ppermute | solution.py:48
  42.3 22.3 %collective-permute-start.2 = (bf16[1,72,1152]{2,1,0:T(8,128)(2,1)}, bf16[1,72,1152]{2,1,0:T(8,128)(2,1)S(1)}, u32[]{:S(2)}, u32[]{:S(2)}) collective-permute-start(bf16[1,72,1152]{2,1,0:T(8,128)(2,1)} %collective-permute-done), channel_id=1, source_target_pairs={{0,32},{16,48},{32,64},{48,80},{64,96},{80,112},{96,128},{112,144}... | collective-permute-start | bytes 497672 | tf_op jit(solution)/shard_map/ppermute | solution.py:48
  45.2 24.6 %collective-permute-start.3 = (bf16[1,72,1152]{2,1,0:T(8,128)(2,1)}, bf16[1,72,1152]{2,1,0:T(8,128)(2,1)S(1)}, u32[]{:S(2)}, u32[]{:S(2)}) collective-permute-start(bf16[1,72,1152]{2,1,0:T(8,128)(2,1)} %collective-permute-done.1), channel_id=1, source_target_pairs={{0,224},{16,240},{32,0},{48,16},{64,32},{80,48},{96,64},{112,80},{... | collective-permute-start | bytes 497672 | tf_op jit(solution)/shard_map/ppermute | solution.py:48
  53.2 8.8 %collective-permute-start.10 = (bf16[1,72,1152]{2,1,0:T(8,128)(2,1)}, bf16[1,72,1152]{2,1,0:T(8,128)(2,1)S(1)}, u32[]{:S(2)}, u32[]{:S(2)}) collective-permute-start(bf16[1,72,1152]{2,1,0:T(8,128)(2,1)} %collective-permute-done.9), channel_id=1, source_target_pairs={{0,32},{16,48},{32,64},{48,80},{64,96},{80,112},{96,128},{112,144}... | collective-permute-start | bytes 497672 | tf_op jit(solution)/shard_map/ppermute | solution.py:48
  55.1 16.6 %collective-permute-start.11 = (bf16[1,72,1152]{2,1,0:T(8,128)(2,1)}, bf16[1,72,1152]{2,1,0:T(8,128)(2,1)S(1)}, u32[]{:S(2)}, u32[]{:S(2)}) collective-permute-start(bf16[1,72,1152]{2,1,0:T(8,128)(2,1)} %collective-permute-done.9), channel_id=1, source_target_pairs={{0,224},{16,240},{32,0},{48,16},{64,32},{80,48},{96,64},{112,80},{... | collective-permute-start | bytes 497672 | tf_op jit(solution)/shard_map/ppermute | solution.py:48
  62.0 15.6 %collective-permute-start.22 = (bf16[2,72,576]{2,1,0:T(8,128)(2,1)S(1)}, bf16[2,72,576]{2,1,0:T(8,128)(2,1)S(1)}, u32[]{:S(2)}, u32[]{:S(2)}) collective-permute-start(bf16[2,72,576]{2,1,0:T(8,128)(2,1)S(1)} %collective-permute-done.20), channel_id=1, source_target_pairs={{0,32},{16,48},{32,64},{48,80},{64,96},{80,112},{96,128},{112,144}... | collective-permute-start | bytes 497672 | tf_op jit(solution)/shard_map/ppermute | solution.py:48
  64.6 14.9 %collective-permute-start.23 = (bf16[2,72,576]{2,1,0:T(8,128)(2,1)S(1)}, bf16[2,72,576]{2,1,0:T(8,128)(2,1)S(1)}, u32[]{:S(2)}, u32[]{:S(2)}) collective-permute-start(bf16[2,72,576]{2,1,0:T(8,128)(2,1)S(1)} %collective-permute-done.21), channel_id=1, source_target_pairs={{0,224},{16,240},{32,0},{48,16},{64,32},{80,48},{96,64},{112,80},{... | collective-permute-start | bytes 497672 | tf_op jit(solution)/shard_map/ppermute | solution.py:48
  69.8 18.9 %collective-permute-start.4 = (bf16[1,72,1152]{2,1,0:T(8,128)(2,1)S(1)}, bf16[1,72,1152]{2,1,0:T(8,128)(2,1)S(1)}, u32[]{:S(2)}, u32[]{:S(2)}) collective-permute-start(bf16[1,72,1152]{2,1,0:T(8,128)(2,1)S(1)} %collective-permute-done.2), channel_id=1, source_target_pairs={{0,32},{16,48},{32,64},{48,80},{64,96},{80,112},{96,128},{112,144}... | collective-permute-start | bytes 497672 | tf_op jit(solution)/shard_map/ppermute | solution.py:48
  71.8 22.1 %collective-permute-start.5 = (bf16[1,72,1152]{2,1,0:T(8,128)(2,1)S(1)}, bf16[1,72,1152]{2,1,0:T(8,128)(2,1)S(1)}, u32[]{:S(2)}, u32[]{:S(2)}) collective-permute-start(bf16[1,72,1152]{2,1,0:T(8,128)(2,1)S(1)} %collective-permute-done.3), channel_id=1, source_target_pairs={{0,224},{16,240},{32,0},{48,16},{64,32},{80,48},{96,64},{112,80},{... | collective-permute-start | bytes 497672 | tf_op jit(solution)/shard_map/ppermute | solution.py:48
  77.6 8.4 %collective-permute-start.12 = (bf16[1,72,1152]{2,1,0:T(8,128)(2,1)S(1)}, bf16[1,72,1152]{2,1,0:T(8,128)(2,1)S(1)}, u32[]{:S(2)}, u32[]{:S(2)}) collective-permute-start(bf16[1,72,1152]{2,1,0:T(8,128)(2,1)S(1)} %collective-permute-done.10), channel_id=1, source_target_pairs={{0,32},{16,48},{32,64},{48,80},{64,96},{80,112},{96,128},{112,144}... | collective-permute-start | bytes 497672 | tf_op jit(solution)/shard_map/ppermute | solution.py:48
  79.6 16.3 %collective-permute-start.13 = (bf16[1,72,1152]{2,1,0:T(8,128)(2,1)S(1)}, bf16[1,72,1152]{2,1,0:T(8,128)(2,1)S(1)}, u32[]{:S(2)}, u32[]{:S(2)}) collective-permute-start(bf16[1,72,1152]{2,1,0:T(8,128)(2,1)S(1)} %collective-permute-done.11), channel_id=1, source_target_pairs={{0,224},{16,240},{32,0},{48,16},{64,32},{80,48},{96,64},{112,80},{... | collective-permute-start | bytes 497672 | tf_op jit(solution)/shard_map/ppermute | solution.py:48
  86.0 15.6 %collective-permute-start.24 = (bf16[2,72,576]{2,1,0:T(8,128)(2,1)S(1)}, bf16[2,72,576]{2,1,0:T(8,128)(2,1)S(1)}, u32[]{:S(2)}, u32[]{:S(2)}) collective-permute-start(bf16[2,72,576]{2,1,0:T(8,128)(2,1)S(1)} %collective-permute-done.22), channel_id=1, source_target_pairs={{0,32},{16,48},{32,64},{48,80},{64,96},{80,112},{96,128},{112,144}... | collective-permute-start | bytes 497672 | tf_op jit(solution)/shard_map/ppermute | solution.py:48
  88.7 15.0 %collective-permute-start.25 = (bf16[2,72,576]{2,1,0:T(8,128)(2,1)S(1)}, bf16[2,72,576]{2,1,0:T(8,128)(2,1)S(1)}, u32[]{:S(2)}, u32[]{:S(2)}) collective-permute-start(bf16[2,72,576]{2,1,0:T(8,128)(2,1)S(1)} %collective-permute-done.23), channel_id=1, source_target_pairs={{0,224},{16,240},{32,0},{48,16},{64,32},{80,48},{96,64},{112,80},{... | collective-permute-start | bytes 497672 | tf_op jit(solution)/shard_map/ppermute | solution.py:48
  93.8 15.0 %collective-permute-start.6 = (bf16[1,72,640]{2,1,0:T(8,128)(2,1)S(1)}, bf16[1,72,640]{2,1,0:T(8,128)(2,1)S(1)}, u32[]{:S(2)}, u32[]{:S(2)}) collective-permute-start(bf16[1,72,640]{2,1,0:T(8,128)(2,1)S(1)} %slice.224), channel_id=1, source_target_pairs={{0,32},{16,48},{32,64},{48,80},{64,96},{80,112},{96,128},{112,144}... | collective-permute-start | bytes 276488 | tf_op jit(solution)/shard_map/ppermute | solution.py:48
  95.8 15.0 %collective-permute-start.7 = (bf16[1,72,512]{2,1,0:T(8,128)(2,1)S(1)}, bf16[1,72,512]{2,1,0:T(8,128)(2,1)S(1)}, u32[]{:S(2)}, u32[]{:S(2)}) collective-permute-start(bf16[1,72,512]{2,1,0:T(8,128)(2,1)S(1)} %slice.225), channel_id=1, source_target_pairs={{0,224},{16,240},{32,0},{48,16},{64,32},{80,48},{96,64},{112,80},{... | collective-permute-start | bytes 221192 | tf_op jit(solution)/shard_map/ppermute | solution.py:48
  101.7 14.3 %collective-permute-start.14 = (bf16[1,72,1152]{2,1,0:T(8,128)(2,1)S(1)}, bf16[1,72,1152]{2,1,0:T(8,128)(2,1)S(1)}, u32[]{:S(2)}, u32[]{:S(2)}) collective-permute-start(bf16[1,72,1152]{2,1,0:T(8,128)(2,1)S(1)} %collective-permute-done.12), channel_id=1, source_target_pairs={{0,32},{16,48},{32,64},{48,80},{64,96},{80,112},{96,128},{112,144}... | collective-permute-start | bytes 497672 | tf_op jit(solution)/shard_map/ppermute | solution.py:48
  103.6 15.0 %collective-permute-start.15 = (bf16[1,72,1152]{2,1,0:T(8,128)(2,1)S(1)}, bf16[1,72,1152]{2,1,0:T(8,128)(2,1)S(1)}, u32[]{:S(2)}, u32[]{:S(2)}) collective-permute-start(bf16[1,72,1152]{2,1,0:T(8,128)(2,1)S(1)} %collective-permute-done.13), channel_id=1, source_target_pairs={{0,224},{16,240},{32,0},{48,16},{64,32},{80,48},{96,64},{112,80},{... | collective-permute-start | bytes 497672 | tf_op jit(solution)/shard_map/ppermute | solution.py:48
  108.9 12.4 %collective-permute-start.26 = (bf16[2,72,384]{2,1,0:T(8,128)(2,1)S(1)}, bf16[2,72,384]{2,1,0:T(8,128)(2,1)S(1)}, u32[]{:S(2)}, u32[]{:S(2)}) collective-permute-start(bf16[2,72,384]{2,1,0:T(8,128)(2,1)S(1)} %slice.233), channel_id=1, source_target_pairs={{0,32},{16,48},{32,64},{48,80},{64,96},{80,112},{96,128},{112,144}... | collective-permute-start | bytes 331784 | tf_op jit(solution)/shard_map/ppermute | solution.py:48
  110.8 15.6 %collective-permute-start.27 = (bf16[2,72,192]{2,1,0:T(8,128)(2,1)S(1)}, bf16[2,72,192]{2,1,0:T(8,128)(2,1)S(1)}, u32[]{:S(2)}, u32[]{:S(2)}) collective-permute-start(bf16[2,72,192]{2,1,0:T(8,128)(2,1)S(1)} %slice.234), channel_id=1, source_target_pairs={{0,224},{16,240},{32,0},{48,16},{64,32},{80,48},{96,64},{112,80},{... | collective-permute-start | bytes 165896 | tf_op jit(solution)/shard_map/ppermute | solution.py:48
  116.0 51.5 %collective-permute-start.8 = (bf16[1,8,72,1152]{3,2,1,0:T(8,128)(2,1)S(1)}, bf16[1,8,72,1152]{3,2,1,0:T(8,128)(2,1)}, u32[]{:S(2)}, u32[]{:S(2)}) collective-permute-start(bf16[1,8,72,1152]{3,2,1,0:T(8,128)(2,1)S(1)} %bitcast_dynamic-update-slice_fusion.34), channel_id=1, source_target_pairs={{0,16},{16,0},{32,48},{48,32},{64,80},{80,64},{96,112},{112,96},{1... | collective-permute-start | bytes 3981320 | tf_op jit(solution)/shard_map/ppermute | solution.py:52
  118.6 9.8 %collective-permute-start.16 = (bf16[1,72,640]{2,1,0:T(8,128)(2,1)S(1)}, bf16[1,72,640]{2,1,0:T(8,128)(2,1)S(1)}, u32[]{:S(2)}, u32[]{:S(2)}) collective-permute-start(bf16[1,72,640]{2,1,0:T(8,128)(2,1)S(1)} %slice.227), channel_id=1, source_target_pairs={{0,32},{16,48},{32,64},{48,80},{64,96},{80,112},{96,128},{112,144}... | collective-permute-start | bytes 276488 | tf_op jit(solution)/shard_map/ppermute | solution.py:48
  126.5 42.8 %collective-permute-start.28 = (bf16[2,8,72,576]{3,2,1,0:T(8,128)(2,1)S(1)}, bf16[2,8,72,576]{3,2,1,0:T(8,128)(2,1)}, u32[]{:S(2)}, u32[]{:S(2)}) collective-permute-start(bf16[2,8,72,576]{3,2,1,0:T(8,128)(2,1)S(1)} %bitcast_dynamic-update-slice_fusion.32), channel_id=1, source_target_pairs={{0,16},{16,0},{32,48},{48,32},{64,80},{80,64},{96,112},{112,96},{1... | collective-permute-start | bytes 3981320 | tf_op jit(solution)/shard_map/ppermute | solution.py:52
  129.7 41.4 %collective-permute-start.18 = (bf16[1,8,72,1152]{3,2,1,0:T(8,128)(2,1)}, bf16[1,8,72,1152]{3,2,1,0:T(8,128)(2,1)}, u32[]{:S(2)}, u32[]{:S(2)}) collective-permute-start(bf16[1,8,72,1152]{3,2,1,0:T(8,128)(2,1)} %bitcast_dynamic-update-slice_fusion.33), channel_id=1, source_target_pairs={{0,16},{16,0},{32,48},{48,32},{64,80},{80,64},{96,112},{112,96},{1... | collective-permute-start | bytes 3981320 | tf_op jit(solution)/shard_map/ppermute | solution.py:52
  148.9 9.3 %collective-permute-start.38 = (f32[1,32]{1,0:T(1,128)S(1)}, f32[1,32]{1,0:T(1,128)S(1)}, u32[]{:S(2)}, u32[]{:S(2)}) collective-permute-start(f32[1,32]{1,0:T(1,128)S(1)} %add.523), channel_id=1, source_target_pairs={{0,128},{16,144},{32,160},{48,176},{64,192},{80,208},{96,224},{112... | collective-permute-start | bytes 392 | tf_op jit(solution)/shard_map/ppermute | solution.py:52
  158.2 9.3 %collective-permute-start.39 = (f32[1,32]{1,0:T(1,128)S(1)}, f32[1,32]{1,0:T(1,128)S(1)}, u32[]{:S(2)}, u32[]{:S(2)}) collective-permute-start(f32[1,32]{1,0:T(1,128)S(1)} %add.524), channel_id=1, source_target_pairs={{0,256},{16,272},{32,288},{48,304},{64,320},{80,336},{96,352},{112... | collective-permute-start | bytes 392 | tf_op jit(solution)/shard_map/ppermute | solution.py:52
  178.8 14.3 %collective-permute-start.29 = (bf16[64,1152]{1,0:T(8,128)(2,1)S(1)}, bf16[64,1152]{1,0:T(8,128)(2,1)S(1)}, u32[]{:S(2)}, u32[]{:S(2)}) collective-permute-start(bf16[64,1152]{1,0:T(8,128)(2,1)S(1)} %get-tuple-element.29), channel_id=1, source_target_pairs={{0,1},{1,2},{2,3},{3,0},{4,5},{5,6},{6,7},{7,4},{8,9},{9,10},{10,1... | collective-permute-start | bytes 442376 | tf_op jit(solution)/shard_map/ppermute | solution.py:57
  182.2 12.9 %collective-permute-start.31 = (bf16[64,1152]{1,0:T(8,128)(2,1)S(1)}, bf16[64,1152]{1,0:T(8,128)(2,1)S(1)}, u32[]{:S(2)}, u32[]{:S(2)}) collective-permute-start(bf16[64,1152]{1,0:T(8,128)(2,1)S(1)} %get-tuple-element.30), channel_id=1, source_target_pairs={{0,3},{1,0},{2,1},{3,2},{4,7},{5,4},{6,5},{7,6},{8,11},{9,8},{10,9... | collective-permute-start | bytes 442376 | tf_op jit(solution)/shard_map/ppermute | solution.py:57
  186.0 14.4 %collective-permute-start.46 = (bf16[64,1152]{1,0:T(8,128)(2,1)S(1)}, bf16[64,1152]{1,0:T(8,128)(2,1)S(1)}, u32[]{:S(2)}, u32[]{:S(2)}) collective-permute-start(bf16[64,1152]{1,0:T(8,128)(2,1)S(1)} %get-tuple-element.27), channel_id=1, source_target_pairs={{0,1},{1,2},{2,3},{3,0},{4,5},{5,6},{6,7},{7,4},{8,9},{9,10},{10,1... | collective-permute-start | bytes 442376 | tf_op jit(solution)/shard_map/ppermute | solution.py:57
  188.2 14.2 %collective-permute-start.48 = (bf16[64,1152]{1,0:T(8,128)(2,1)S(1)}, bf16[64,1152]{1,0:T(8,128)(2,1)S(1)}, u32[]{:S(2)}, u32[]{:S(2)}) collective-permute-start(bf16[64,1152]{1,0:T(8,128)(2,1)S(1)} %get-tuple-element.28), channel_id=1, source_target_pairs={{0,3},{1,0},{2,1},{3,2},{4,7},{5,4},{6,5},{7,6},{8,11},{9,8},{10,9... | collective-permute-start | bytes 442376 | tf_op jit(solution)/shard_map/ppermute | solution.py:57
  193.2 14.4 %collective-permute-start.30 = (bf16[64,2304]{1,0:T(8,128)(2,1)S(1)}, bf16[64,2304]{1,0:T(8,128)(2,1)S(1)}, u32[]{:S(2)}, u32[]{:S(2)}) collective-permute-start(bf16[64,2304]{1,0:T(8,128)(2,1)S(1)} %pad_maximum_fusion.6), channel_id=1, source_target_pairs={{0,1},{1,2},{2,3},{3,0},{4,5},{5,6},{6,7},{7,4},{8,9},{9,10},{10,1... | collective-permute-start | bytes 884744 | tf_op jit(solution)/shard_map/ppermute | solution.py:57
  195.2 12.4 %collective-permute-start.32 = (bf16[64,2304]{1,0:T(8,128)(2,1)S(1)}, bf16[64,2304]{1,0:T(8,128)(2,1)S(1)}, u32[]{:S(2)}, u32[]{:S(2)}) collective-permute-start(bf16[64,2304]{1,0:T(8,128)(2,1)S(1)} %pad_maximum_fusion.7), channel_id=1, source_target_pairs={{0,3},{1,0},{2,1},{3,2},{4,7},{5,4},{6,5},{7,6},{8,11},{9,8},{10,9... | collective-permute-start | bytes 884744 | tf_op jit(solution)/shard_map/ppermute | solution.py:57
  200.5 10.6 %collective-permute-start.47 = (bf16[64,2304]{1,0:T(8,128)(2,1)S(1)}, bf16[64,2304]{1,0:T(8,128)(2,1)S(1)}, u32[]{:S(2)}, u32[]{:S(2)}) collective-permute-start(bf16[64,2304]{1,0:T(8,128)(2,1)S(1)} %pad_maximum_fusion.8), channel_id=1, source_target_pairs={{0,1},{1,2},{2,3},{3,0},{4,5},{5,6},{6,7},{7,4},{8,9},{9,10},{10,1... | collective-permute-start | bytes 884744 | tf_op jit(solution)/shard_map/ppermute | solution.py:57
  202.5 9.4 %collective-permute-start.49 = (bf16[64,2304]{1,0:T(8,128)(2,1)S(1)}, bf16[64,2304]{1,0:T(8,128)(2,1)S(1)}, u32[]{:S(2)}, u32[]{:S(2)}) collective-permute-start(bf16[64,2304]{1,0:T(8,128)(2,1)S(1)} %pad_maximum_fusion.9), channel_id=1, source_target_pairs={{0,3},{1,0},{2,1},{3,2},{4,7},{5,4},{6,5},{7,6},{8,11},{9,8},{10,9... | collective-permute-start | bytes 884744 | tf_op jit(solution)/shard_map/ppermute | solution.py:57
  215.5 8.1 %collective-permute-start.34 = (bf16[16,2304]{1,0:T(8,128)(2,1)S(1)}, bf16[16,2304]{1,0:T(8,128)(2,1)S(1)}, u32[]{:S(2)}, u32[]{:S(2)}) collective-permute-start(bf16[16,2304]{1,0:T(8,128)(2,1)S(1)} %fusion.71), channel_id=1, source_target_pairs={{0,8},{1,9},{2,10},{3,11},{4,12},{5,13},{6,14},{7,15},{8,0},{9,1},... | collective-permute-start | bytes 221192 | tf_op jit(solution)/shard_map/ppermute | solution.py:61
  220.1 9.3 %collective-permute-start.51 = (bf16[16,2304]{1,0:T(8,128)(2,1)S(1)}, bf16[16,2304]{1,0:T(8,128)(2,1)S(1)}, u32[]{:S(2)}, u32[]{:S(2)}) collective-permute-start(bf16[16,2304]{1,0:T(8,128)(2,1)S(1)} %fusion.72), channel_id=1, source_target_pairs={{0,8},{1,9},{2,10},{3,11},{4,12},{5,13},{6,14},{7,15},{8,0},{9,1},... | collective-permute-start | bytes 221192 | tf_op jit(solution)/shard_map/ppermute | solution.py:61
  231.6 8.2 %collective-permute-start.40 = (bf16[16,2304]{1,0:T(8,128)(2,1)S(1)}, bf16[16,2304]{1,0:T(8,128)(2,1)S(1)}, u32[]{:S(2)}, u32[]{:S(2)}) collective-permute-start(bf16[16,2304]{1,0:T(8,128)(2,1)S(1)} %get-tuple-element.34), channel_id=1, source_target_pairs={{0,8},{1,9},{2,10},{3,11},{4,12},{5,13},{6,14},{7,15},{8,0},{9,1},... | collective-permute-start | bytes 221192 | tf_op jit(solution)/shard_map/ppermute | solution.py:61
  239.8 12.7 %collective-permute-start.41 = (bf16[2,16,2304]{2,1,0:T(8,128)(2,1)S(1)}, bf16[2,16,2304]{2,1,0:T(8,128)(2,1)S(1)}, u32[]{:S(2)}, u32[]{:S(2)}) collective-permute-start(bf16[2,16,2304]{2,1,0:T(8,128)(2,1)S(1)} %maximum_select_fusion.3), channel_id=1, source_target_pairs={{0,4},{1,5},{2,6},{3,7},{4,0},{5,1},{6,2},{7,3},{8,12},{9,13},{10,... | collective-permute-start | bytes 442376 | tf_op jit(solution)/shard_map/ppermute | solution.py:61
  244.9 15.0 %collective-permute-start.54 = (bf16[64,2304]{1,0:T(8,128)(2,1)S(1)}, bf16[64,2304]{1,0:T(8,128)(2,1)S(1)}, u32[]{:S(2)}, u32[]{:S(2)}) collective-permute-start(bf16[64,2304]{1,0:T(8,128)(2,1)S(1)} %bitcast.300), channel_id=1, source_target_pairs={{0,1},{1,2},{2,3},{3,0},{4,5},{5,6},{6,7},{7,4},{8,9},{9,10},{10,1... | collective-permute-start | bytes 884744 | tf_op jit(solution)/shard_map/ppermute | solution.py:57
  246.9 15.0 %collective-permute-start.55 = (bf16[64,2304]{1,0:T(8,128)(2,1)S(1)}, bf16[64,2304]{1,0:T(8,128)(2,1)S(1)}, u32[]{:S(2)}, u32[]{:S(2)}) collective-permute-start(bf16[64,2304]{1,0:T(8,128)(2,1)S(1)} %bitcast.301), channel_id=1, source_target_pairs={{0,3},{1,0},{2,1},{3,2},{4,7},{5,4},{6,5},{7,6},{8,11},{9,8},{10,9... | collective-permute-start | bytes 884744 | tf_op jit(solution)/shard_map/ppermute | solution.py:57
  252.6 14.4 %collective-permute-start.42 = (bf16[64,2304]{1,0:T(8,128)(2,1)S(1)}, bf16[64,2304]{1,0:T(8,128)(2,1)S(1)}, u32[]{:S(2)}, u32[]{:S(2)}) collective-permute-start(bf16[64,2304]{1,0:T(8,128)(2,1)S(1)} %bitcast.303), channel_id=1, source_target_pairs={{0,1},{1,2},{2,3},{3,0},{4,5},{5,6},{6,7},{7,4},{8,9},{9,10},{10,1... | collective-permute-start | bytes 884744 | tf_op jit(solution)/shard_map/ppermute | solution.py:57
  254.5 14.5 %collective-permute-start.43 = (bf16[64,2304]{1,0:T(8,128)(2,1)S(1)}, bf16[64,2304]{1,0:T(8,128)(2,1)S(1)}, u32[]{:S(2)}, u32[]{:S(2)}) collective-permute-start(bf16[64,2304]{1,0:T(8,128)(2,1)S(1)} %bitcast.304), channel_id=1, source_target_pairs={{0,3},{1,0},{2,1},{3,2},{4,7},{5,4},{6,5},{7,6},{8,11},{9,8},{10,9... | collective-permute-start | bytes 884744 | tf_op jit(solution)/shard_map/ppermute | solution.py:57
  260.0 17.4 %collective-permute-start.56 = (bf16[64,1152]{1,0:T(8,128)(2,1)S(1)}, bf16[64,1152]{1,0:T(8,128)(2,1)S(1)}, u32[]{:S(2)}, u32[]{:S(2)}) collective-permute-start(bf16[64,1152]{1,0:T(8,128)(2,1)S(1)} %slice.250), channel_id=1, source_target_pairs={{0,1},{1,2},{2,3},{3,0},{4,5},{5,6},{6,7},{7,4},{8,9},{9,10},{10,1... | collective-permute-start | bytes 442376 | tf_op jit(solution)/shard_map/ppermute | solution.py:57
  261.9 16.0 %collective-permute-start.57 = (bf16[64,1152]{1,0:T(8,128)(2,1)S(1)}, bf16[64,1152]{1,0:T(8,128)(2,1)S(1)}, u32[]{:S(2)}, u32[]{:S(2)}) collective-permute-start(bf16[64,1152]{1,0:T(8,128)(2,1)S(1)} %slice.251), channel_id=1, source_target_pairs={{0,3},{1,0},{2,1},{3,2},{4,7},{5,4},{6,5},{7,6},{8,11},{9,8},{10,9... | collective-permute-start | bytes 442376 | tf_op jit(solution)/shard_map/ppermute | solution.py:57
  267.1 8.2 %collective-permute-start.44 = (bf16[64,1152]{1,0:T(8,128)(2,1)S(1)}, bf16[64,1152]{1,0:T(8,128)(2,1)S(1)}, u32[]{:S(2)}, u32[]{:S(2)}) collective-permute-start(bf16[64,1152]{1,0:T(8,128)(2,1)S(1)} %slice.241), channel_id=1, source_target_pairs={{0,1},{1,2},{2,3},{3,0},{4,5},{5,6},{6,7},{7,4},{8,9},{9,10},{10,1... | collective-permute-start | bytes 442376 | tf_op jit(solution)/shard_map/ppermute | solution.py:57
  292.7 13.7 %collective-permute-start.63 = (bf16[72,352]{1,0:T(8,128)(2,1)S(1)}, bf16[72,352]{1,0:T(8,128)(2,1)S(1)}, u32[]{:S(2)}, u32[]{:S(2)}) collective-permute-start(bf16[72,352]{1,0:T(8,128)(2,1)S(1)} %slice.263), channel_id=1, source_target_pairs={{0,224},{16,240},{32,0},{48,16},{64,32},{80,48},{96,64},{112,80},{... | collective-permute-start | bytes 152072 | tf_op jit(solution)/shard_map/ppermute | solution.py:48
  297.4 20.2 %collective-permute-start.59 = (bf16[72,512]{1,0:T(8,128)(2,1)S(1)}, bf16[72,512]{1,0:T(8,128)(2,1)S(1)}, u32[]{:S(2)}, u32[]{:S(2)}) collective-permute-start(bf16[72,512]{1,0:T(8,128)(2,1)S(1)} %slice.259), channel_id=1, source_target_pairs={{0,32},{16,48},{32,64},{48,80},{64,96},{80,112},{96,128},{112,144}... | collective-permute-start | bytes 221192 | tf_op jit(solution)/shard_map/ppermute | solution.py:48
  299.3 12.3 %collective-permute-start.72 = (bf16[72,352]{1,0:T(8,128)(2,1)S(1)}, bf16[72,352]{1,0:T(8,128)(2,1)S(1)}, u32[]{:S(2)}, u32[]{:S(2)}) collective-permute-start(bf16[72,352]{1,0:T(8,128)(2,1)S(1)} %slice.273), channel_id=1, source_target_pairs={{0,224},{16,240},{32,0},{48,16},{64,32},{80,48},{96,64},{112,80},{... | collective-permute-start | bytes 152072 | tf_op jit(solution)/shard_map/ppermute | solution.py:48
  304.5 9.1 %collective-permute-start.68 = (bf16[72,512]{1,0:T(8,128)(2,1)S(1)}, bf16[72,512]{1,0:T(8,128)(2,1)S(1)}, u32[]{:S(2)}, u32[]{:S(2)}) collective-permute-start(bf16[72,512]{1,0:T(8,128)(2,1)S(1)} %slice.269), channel_id=1, source_target_pairs={{0,32},{16,48},{32,64},{48,80},{64,96},{80,112},{96,128},{112,144}... | collective-permute-start | bytes 221192 | tf_op jit(solution)/shard_map/ppermute | solution.py:48
  306.5 27.1 %collective-permute-start.64 = (bf16[72,864]{1,0:T(8,128)(2,1)S(1)}, bf16[72,864]{1,0:T(8,128)(2,1)S(1)}, u32[]{:S(2)}, u32[]{:S(2)}) collective-permute-start(bf16[72,864]{1,0:T(8,128)(2,1)S(1)} %pad_maximum_fusion.14), channel_id=1, source_target_pairs={{0,224},{16,240},{32,0},{48,16},{64,32},{80,48},{96,64},{112,80},{... | collective-permute-start | bytes 373256 | tf_op jit(solution)/shard_map/ppermute | solution.py:48
  311.7 16.5 %collective-permute-start.73 = (bf16[72,864]{1,0:T(8,128)(2,1)S(1)}, bf16[72,864]{1,0:T(8,128)(2,1)S(1)}, u32[]{:S(2)}, u32[]{:S(2)}) collective-permute-start(bf16[72,864]{1,0:T(8,128)(2,1)S(1)} %pad_maximum_fusion.16), channel_id=1, source_target_pairs={{0,224},{16,240},{32,0},{48,16},{64,32},{80,48},{96,64},{112,80},{... | collective-permute-start | bytes 373256 | tf_op jit(solution)/shard_map/ppermute | solution.py:48
  313.7 8.1 %collective-permute-start.69 = (bf16[72,864]{1,0:T(8,128)(2,1)S(1)}, bf16[72,864]{1,0:T(8,128)(2,1)S(1)}, u32[]{:S(2)}, u32[]{:S(2)}) collective-permute-start(bf16[72,864]{1,0:T(8,128)(2,1)S(1)} %pad_maximum_fusion.15), channel_id=1, source_target_pairs={{0,32},{16,48},{32,64},{48,80},{64,96},{80,112},{96,128},{112,144}... | collective-permute-start | bytes 373256 | tf_op jit(solution)/shard_map/ppermute | solution.py:48
  317.6 8.5 %collective-permute-start.60 = (bf16[72,864]{1,0:T(8,128)(2,1)S(1)}, bf16[72,864]{1,0:T(8,128)(2,1)S(1)}, u32[]{:S(2)}, u32[]{:S(2)}) collective-permute-start(bf16[72,864]{1,0:T(8,128)(2,1)S(1)} %pad_maximum_fusion.13), channel_id=1, source_target_pairs={{0,32},{16,48},{32,64},{48,80},{64,96},{80,112},{96,128},{112,144}... | collective-permute-start | bytes 373256 | tf_op jit(solution)/shard_map/ppermute | solution.py:48
  321.7 9.2 %collective-permute-start.70 = (bf16[72,864]{1,0:T(8,128)(2,1)S(1)}, bf16[72,864]{1,0:T(8,128)(2,1)S(1)}, u32[]{:S(2)}, u32[]{:S(2)}) collective-permute-start(bf16[72,864]{1,0:T(8,128)(2,1)S(1)} %fusion.45), channel_id=1, source_target_pairs={{0,32},{16,48},{32,64},{48,80},{64,96},{80,112},{96,128},{112,144}... | collective-permute-start | bytes 373256 | tf_op jit(solution)/shard_map/ppermute | solution.py:48
  331.0 12.1 %collective-permute-start.74 = (bf16[72,864]{1,0:T(8,128)(2,1)S(1)}, bf16[72,864]{1,0:T(8,128)(2,1)S(1)}, u32[]{:S(2)}, u32[]{:S(2)}) collective-permute-start(bf16[72,864]{1,0:T(8,128)(2,1)S(1)} %get-tuple-element.23), channel_id=1, source_target_pairs={{0,224},{16,240},{32,0},{48,16},{64,32},{80,48},{96,64},{112,80},{... | collective-permute-start | bytes 373256 | tf_op jit(solution)/shard_map/ppermute | solution.py:48
  334.4 13.3 %collective-permute-start.65 = (bf16[72,864]{1,0:T(8,128)(2,1)S(1)}, bf16[72,864]{1,0:T(8,128)(2,1)S(1)}, u32[]{:S(2)}, u32[]{:S(2)}) collective-permute-start(bf16[72,864]{1,0:T(8,128)(2,1)S(1)} %get-tuple-element.18), channel_id=1, source_target_pairs={{0,224},{16,240},{32,0},{48,16},{64,32},{80,48},{96,64},{112,80},{... | collective-permute-start | bytes 373256 | tf_op jit(solution)/shard_map/ppermute | solution.py:48
  336.5 16.4 %collective-permute-start.62 = (bf16[72,864]{1,0:T(8,128)(2,1)S(1)}, bf16[72,864]{1,0:T(8,128)(2,1)S(1)}, u32[]{:S(2)}, u32[]{:S(2)}) collective-permute-start(bf16[72,864]{1,0:T(8,128)(2,1)S(1)} %get-tuple-element.17), channel_id=1, source_target_pairs={{0,32},{16,48},{32,64},{48,80},{64,96},{80,112},{96,128},{112,144}... | collective-permute-start | bytes 373256 | tf_op jit(solution)/shard_map/ppermute | solution.py:48
  340.4 9.3 %collective-permute-start.71 = (bf16[72,864]{1,0:T(8,128)(2,1)S(1)}, bf16[72,864]{1,0:T(8,128)(2,1)S(1)}, u32[]{:S(2)}, u32[]{:S(2)}) collective-permute-start(bf16[72,864]{1,0:T(8,128)(2,1)S(1)} %get-tuple-element.22), channel_id=1, source_target_pairs={{0,32},{16,48},{32,64},{48,80},{64,96},{80,112},{96,128},{112,144}... | collective-permute-start | bytes 373256 | tf_op jit(solution)/shard_map/ppermute | solution.py:48
  350.6 11.2 %collective-permute-start.76 = (bf16[72,864]{1,0:T(8,128)(2,1)S(1)}, bf16[72,864]{1,0:T(8,128)(2,1)S(1)}, u32[]{:S(2)}, u32[]{:S(2)}) collective-permute-start(bf16[72,864]{1,0:T(8,128)(2,1)S(1)} %fusion.48), channel_id=1, source_target_pairs={{0,256},{16,272},{32,288},{48,304},{64,320},{80,336},{96,352},{112... | collective-permute-start | bytes 373256 | tf_op jit(solution)/shard_map/ppermute | solution.py:52
  (30 other events, 399.5 us)
